TPU v7x, 128 devices: a whole 4x4x4 slice. The times are simulated.
128 devices in a mesh: group: 4 (over z), curve: 32 (over x, y, core).
Axes of the slice: x: 4, y: 4, z: 4, core: 2. Of those that a mesh axis runs over, the one named last changes fastest.
Arguments:
- moisture: float32 [72, 16, 131072], P(None, None, ('group', 'curve')), may hold values from -6 to 6
- jacobian: float32 [131072], P(('group', 'curve')), may hold values from 0.5 to 2
- partners: int32 [2, 131072], P(None, ('group', 'curve')), may hold values from 0 to 131071, as said below
- daylit: int32 [131072], P(('group', 'curve')), may hold values from 0 to 1, as said below
- cos_zenith: float32 [131072], P(('group', 'curve')), may hold values from 0.05 to 1
- albedo: float32 [131072], P(('group', 'curve')), may hold values from 0.05 to 0.8
- absorb: float32 [112, 72], replicated, may hold values from 0.002 to 0.2
- rayleigh: float32 [112], replicated, may hold values from 0.005 to 0.05
- solar: float32 [112], replicated, may hold values from 0.002 to 0.02
Outputs:
- moisture_new: float32 [72, 16, 131072], P(None, None, ('group', 'curve'))
- heating: float32 [72, 131072], P(None, ('group', 'curve'))
Inputs may be any that keep to these rules, and one draw needn't show every extreme that they name: partners pairs elements of one group with each other (partner of partner is the element itself, never the element itself, the same for row 0 and row 1 separately); the partner of a group-local position p lies in the same block of 1024 consecutive positions that start at 512 + a multiple of 1024, taken cyclically in the group. Exactly 65536 elements are daylit in all; the groups' counts differ; within each group the daylit elements form one to three runs along the curve, and a run may wrap around the group's end.
All inputs are finite; a program needn't handle non-finite values.
Results may differ from a plain program's by a relative error of at most 0.000094.
Values sent between devices are 32-bit elements; how exact they have to be, the bound alone decides.
A program may use at most 192 MiB of HBM per device.

v0:
```python
import jax
import jax.numpy as jnp
import numpy as np
from jax import lax
from jax.sharding import PartitionSpec as P

edge_nodes = np.array([4, 8, 7, 11, 1, 2, 13, 14])
STEP_SIZE = 0.02
DIFFUSE_FACTOR = 1.66
highest = lax.Precision.HIGHEST


def extended_2(cells, sides, width):
    for axis, dim in sides:
        count = lax.axis_size(axis)
        head = lax.slice_in_dim(cells, 0, width, axis=dim)
        tail = lax.slice_in_dim(cells, cells.shape[dim] - width, cells.shape[dim], axis=dim)
        cells = jnp.concatenate(
            [
                lax.ppermute(tail, axis, [(i, (i + 1) % count) for i in range(count)]),
                cells,
                lax.ppermute(head, axis, [((i + 1) % count, i) for i in range(count)]),
            ],
            axis=dim,
        )
    return cells


def gll_tables():
    points = np.array([-1.0, -1.0 / np.sqrt(5.0), 1.0 / np.sqrt(5.0), 1.0])
    weights = np.array([1.0 / 6.0, 5.0 / 6.0, 5.0 / 6.0, 1.0 / 6.0])
    on_diag = np.eye(4, dtype=bool)
    diffs = np.where(on_diag, 1.0, points[:, None] - points[None, :])
    products = np.prod(diffs, axis=1)
    derivative = products[:, None] / products[None, :] / diffs
    inverse_diff = np.where(on_diag, 0.0, 1.0 / diffs)
    derivative = np.where(on_diag, inverse_diff.sum(axis=1)[:, None], derivative)
    second_diff = derivative @ derivative
    node_weight = weights[:, None] * weights[None, :]
    return (jnp.asarray(second_diff, jnp.float32), jnp.asarray(node_weight, jnp.float32))


def radiate(column_q, cos_zenith, albedo, absorb, rayleigh, solar):
    levels = column_q.shape[0]
    layer_tau = absorb.T[:, :, None] * (column_q * column_q)[:, None, :] + rayleigh[None, :, None]
    column_depth = jnp.cumsum(layer_tau, axis=0)
    top_flux = solar[:, None] * cos_zenith[None, :]
    direct_all = top_flux[None] * jnp.exp(-(column_depth - layer_tau) / cos_zenith[None, None, :])
    bottom_flux = top_flux * jnp.exp(-column_depth[-1] / cos_zenith[None, :])
    diffuse = jnp.exp(-DIFFUSE_FACTOR * layer_tau)
    reflect = 0.5 * (rayleigh[None, :, None] / layer_tau) * (1.0 - diffuse)

    def climb_up(below, layer):
        refl_now, diff_now = layer
        above = refl_now + diff_now * diff_now * below / (1.0 - refl_now * below)
        return (above, above)

    start_albedo = jnp.broadcast_to(albedo[None, :], top_flux.shape)
    _, level_albedo = lax.scan(climb_up, start_albedo, (reflect, diffuse), reverse=True)
    net_top = direct_all * (1.0 - level_albedo)
    net_bottom = bottom_flux * (1.0 - albedo[None, :])
    net_next = jnp.concatenate([net_top[1:], net_bottom[None]], axis=0)
    return levels * jnp.sum(net_top - net_next, axis=1)


def radiate_blocks(column_q, cos_zenith, albedo, absorb, rayleigh, solar):
    levels, columns = column_q.shape
    block_size = min(columns, 512)
    block_count = columns // block_size
    q_blocks = column_q.reshape(levels, block_count, block_size).transpose(1, 0, 2)

    def one_block(block):
        return radiate(block[0], block[1], block[2], absorb, rayleigh, solar)

    results = lax.map(
        one_block,
        (
            q_blocks,
            cos_zenith.reshape(block_count, block_size),
            albedo.reshape(block_count, block_size),
        ),
    )
    return results.transpose(1, 0, 2).reshape(levels, columns)


def shards(moisture, jacobian, partners, daylit, cos_zenith, albedo, absorb, rayleigh, solar):
    levels = moisture.shape[0]
    elements = moisture.shape[2]
    half_width = elements // 2
    e_group = elements * lax.axis_size("curve")
    first_elem = lax.axis_index("curve") * elements
    second_diff, node_weight = gll_tables()
    nodal = moisture.reshape(levels, 4, 4, elements)
    second_x = jnp.einsum("ik,lkjn->lijn", second_diff, nodal, precision=highest)
    second_y = jnp.einsum("jk,likn->lijn", second_diff, nodal, precision=highest)
    weighted = (node_weight[None, :, :, None] * (second_x + second_y)).reshape(levels, 16, elements)
    masses = (node_weight[:, :, None] * jacobian[None, None, :]).reshape(16, elements)
    stacked = jnp.concatenate([weighted[:, edge_nodes, :], masses[edge_nodes][None]], axis=0)
    extended = extended_2(stacked, (("curve", 2),), half_width)
    west_side = extended[:, 2:4, half_width - 1 : half_width - 1 + elements]
    east_side = extended[:, 0:2, half_width + 1 : half_width + 1 + elements]
    crossed = extended[:, 4:8]
    rel_index = (partners % e_group - first_elem + half_width) % e_group
    south_side = jnp.take(crossed[:, 0:2], rel_index[0], axis=2)[:, ::-1]
    north_side = jnp.take(crossed[:, 2:4], rel_index[1], axis=2)[:, ::-1]
    partner_sum = jnp.concatenate([west_side, east_side, south_side, north_side], axis=1)
    assembled = stacked + partner_sum
    edge_ratio = assembled[:levels] / assembled[levels][None]
    tendency = weighted / masses[None]
    tendency = tendency.at[:, edge_nodes, :].set(edge_ratio)
    moisture_new = moisture + STEP_SIZE * tendency
    column_q = jnp.sum(node_weight.reshape(16)[None, :, None] * moisture_new, axis=1) / 4.0
    heat_all = radiate_blocks(column_q, cos_zenith, albedo, absorb, rayleigh, solar)
    heating = jnp.where(daylit[None, :] == 1, heat_all, jnp.float32(0.0))
    return (moisture_new, heating)


def solution(mesh):
    placed = (
        P(None, None, ("group", "curve")),
        P(("group", "curve")),
        P(None, ("group", "curve")),
        P(("group", "curve")),
        P(("group", "curve")),
        P(("group", "curve")),
        P(),
        P(),
        P(),
    )
    return jax.shard_map(
        shards,
        mesh=mesh,
        in_specs=placed,
        out_specs=(P(None, None, ("group", "curve")), P(None, ("group", "curve"))),
        check_vma=False,
    )
```

profile of v0, /device:TPU:0, one launch (start us, length us, event | category | flops | bytes accessed | tf_op | source)
XLA Modules:
  0.0 656.8 jit_solution(2616007375816346317)
XLA Ops:
  0.6 6.3 reshape.181
  6.9 10.3 %fusion.37 = f32[4,72,4,1024]{3,0,2,1:T(4,128)S(1)} fusion(f32[4,4,1,1]{1,0,3,2:T(4,128)S(1)} %copy-done.6, f32[72,4,4,1024]{3,2,1,0:T(4,128)} %reshape.181), kind=kOutput, calls=%fused_computation.93 | convolution fusion | flops 56623104 | bytes 9437248 | tf_op jit(solution)/shard_map/jk,likn->lijn/dot_general | solution.py:95
  17.3 13.5 %fusion.13 = f32[72,4,4,1024]{3,1,2,0:T(4,128)S(1)} fusion(f32[4,72,4,1024]{3,0,2,1:T(4,128)S(1)} %fusion.37, f32[4,4]{0,1:T(4,128)S(1)} %copy-done.13, f32[4,4,1,1]{1,0,3,2:T(4,128)S(1)} %copy-done.6, f32[72,4,4,1024]{3,2,1,0:T(4,128)S(1)} %copy-done), kind=kOutput, calls=%fused_computation.38 | convolution fusion | flops 58982400 | bytes 14155904 | tf_op jit(solution)/shard_map/ik,lkjn->lijn/dot_general | solution.py:94
  30.8 4.9 copy.45
  43.3 5.1 collective-permute-start.1
  49.1 5.5 broadcast_divide_fusion
  54.6 6.4 collective-permute-done
  72.7 9.1 %gather_fusion.2 = f32[1024,73,2]{1,2,0:T(2,128)} fusion(f32[73,2,2048]{0,1,2:T(2,128)} %copy.52, s32[1024]{0:T(1024)S(1)} %fusion.33), kind=kCustom, calls=%fused_computation.clone | custom fusion | bytes 1200128 | tf_op jit(solution)/shard_map/jit(_take)/gather | solution.py:104
  89.3 9.1 %gather_fusion.3 = f32[1024,73,2]{1,2,0:T(2,128)} fusion(f32[73,2,2048]{0,1,2:T(2,128)} %copy.54, s32[1024]{0:T(1024)S(1)} %fusion.34), kind=kCustom, calls=%fused_computation.1.clone | custom fusion | bytes 1200128 | tf_op jit(solution)/shard_map/jit(_take)/gather | solution.py:105
  113.3 7.2 %multiply_reduce_fusion = (f32[72,1024]{1,0:T(8,128)S(1)}, f32[72,16,1024]{2,0,1:T(8,128)S(1)}) fusion(f32[16]{0:T(128)S(1)} %copy-done.14, f32[72,16,1024]{2,0,1:T(8,128)} %scatter_fusion, f32[72,16,1024]{2,1,0:T(8,128)} %param.21), kind=kLoop, calls=%fused_computation.42 | loop fusion | flops 4644864 | bytes 14450752 | tf_op jit(solution)/shard_map/reduce_sum | solution.py:112
  120.5 4.9 copy.59
  125.7 529.9 %while.43 = (s32[]{:T(128)}, f32[2,72,512]{2,1,0:T(8,128)S(1)}, f32[112]{0:T(128)S(1)}, f32[2,512]{1,0:T(2,128)S(1)}, f32[112,72]{0,1:T(8,128)S(1)}, /*index=5*/...) while((s32[]{:T(128)}, f32[2,72,512]{2,1,0:T(8,128)S(1)}, ...), condition=%wide.region_7.9_spmd, body=%wide.region_2.8_spmd.sunk | while | flops 376443392 | bytes 217945232 | solution.py:75
  146.2 12.2 %multiply_exponential_fusion.2 = (f32[72,112,512]{2,1,0:T(8,128)}, f32[72,112,512]{2,1,0:T(8,128)}) fusion(f32[112]{0:T(128)S(1)} %get-tuple-element.520, f32[72,512]{1,0:T(8,128)S(1)} %fusion.44, f32[72,112]{1,0:T(8,128)S(1)} %bitcast.75), kind=kLoop, calls=%fused_computation.15.clone.2 | loop fusion | flops 28901376 | bytes 33210304 | tf_op jit(solution)/shard_map/while/body/eval_jaxpr/exp | solution.py:50
  158.4 7.8 %broadcast.271 = f32[72,112,512]{2,1,0:T(8,128)} broadcast(f32[]{:T(128)} %constant.164.clone.3..sunk), dimensions={} | broadcast | bytes 16515076 | tf_op jit(solution)/shard_map/broadcast.172
  166.2 135.9 %while.44 = (s32[]{:T(128)}, f32[112,512]{1,0:T(8,128)S(1)}, f32[72,112,512]{2,1,0:T(8,128)}, f32[72,112,512]{2,1,0:T(8,128)}, f32[72,112,512]{2,1,0:T(8,128)}, /*index=5*/s32[]{:T(128)}, s32[]{:T(128)}) while((s32[]{:T(128)}, f32[112,512]{1,0:T(8,128)S(1)}, f32[72,112,512]{2,1,0:T(8,128)}, f32[72,112,512]{2,1,0:T(8,128)}, ...), condition=%wide.region_5.6_spmd, body=%wide.region_4.5_spmd.sunk | while | flops 344067 | bytes 1146973 | solution.py:59
  302.2 82.9 %subtract_multiply_fusion.3 = (f32[72,112,512]{2,1,0:T(8,128)}, f32[72,112,512]{2,1,0:T(8,128)}) fusion(f32[72,112,512]{2,1,0:T(8,128)} %get-tuple-element.454, f32[512]{0:T(512)S(1)} %bitcast.80, f32[112]{0:T(128)S(1)} %get-tuple-element.520, f32[72,512]{1,0:T(8,128)S(1)} %fusion.44, f32[72,112]{1,0:T(8,128)S(1)} %bitcast.76, ...), kind=kOutput, calls=%fused_computation.13.clone.1 | output fusion | flops 334430208 | bytes 49956800 | tf_op jit(solution)/shard_map/while/body/eval_jaxpr/jit(cumsum)/reduce_window_sum | solution.py:46
  385.1 7.7 %slice.110 = f32[71,112,512]{2,1,0:T(8,128)S(1)} slice(f32[72,112,512]{2,1,0:T(8,128)} %get-tuple-element.456), slice={[1:72], [0:112], [0:512]} | slice | bytes 32571392 | tf_op jit(solution)/shard_map/while/body/eval_jaxpr/slice | solution.py:62
  395.7 5.0 fusion.46
  401.0 12.2 %multiply_exponential_fusion.2 = (f32[72,112,512]{2,1,0:T(8,128)}, f32[72,112,512]{2,1,0:T(8,128)}) fusion(f32[112]{0:T(128)S(1)} %get-tuple-element.520, f32[72,512]{1,0:T(8,128)S(1)} %fusion.44, f32[72,112]{1,0:T(8,128)S(1)} %bitcast.75), kind=kLoop, calls=%fused_computation.15.clone.2 | loop fusion | flops 28901376 | bytes 33210304 | tf_op jit(solution)/shard_map/while/body/eval_jaxpr/exp | solution.py:50
  413.2 7.8 %broadcast.271 = f32[72,112,512]{2,1,0:T(8,128)} broadcast(f32[]{:T(128)} %constant.164.clone.3..sunk), dimensions={} | broadcast | bytes 16515076 | tf_op jit(solution)/shard_map/broadcast.172
  421.0 135.9 %while.44 = (s32[]{:T(128)}, f32[112,512]{1,0:T(8,128)S(1)}, f32[72,112,512]{2,1,0:T(8,128)}, f32[72,112,512]{2,1,0:T(8,128)}, f32[72,112,512]{2,1,0:T(8,128)}, /*index=5*/s32[]{:T(128)}, s32[]{:T(128)}) while((s32[]{:T(128)}, f32[112,512]{1,0:T(8,128)S(1)}, f32[72,112,512]{2,1,0:T(8,128)}, f32[72,112,512]{2,1,0:T(8,128)}, ...), condition=%wide.region_5.6_spmd, body=%wide.region_4.5_spmd.sunk | while | flops 344067 | bytes 1146973 | solution.py:59
  557.0 82.9 %subtract_multiply_fusion.3 = (f32[72,112,512]{2,1,0:T(8,128)}, f32[72,112,512]{2,1,0:T(8,128)}) fusion(f32[72,112,512]{2,1,0:T(8,128)} %get-tuple-element.454, f32[512]{0:T(512)S(1)} %bitcast.80, f32[112]{0:T(128)S(1)} %get-tuple-element.520, f32[72,512]{1,0:T(8,128)S(1)} %fusion.44, f32[72,112]{1,0:T(8,128)S(1)} %bitcast.76, ...), kind=kOutput, calls=%fused_computation.13.clone.1 | output fusion | flops 334430208 | bytes 49956800 | tf_op jit(solution)/shard_map/while/body/eval_jaxpr/jit(cumsum)/reduce_window_sum | solution.py:46
  639.9 7.7 %slice.110 = f32[71,112,512]{2,1,0:T(8,128)S(1)} slice(f32[72,112,512]{2,1,0:T(8,128)} %get-tuple-element.456), slice={[1:72], [0:112], [0:512]} | slice | bytes 32571392 | tf_op jit(solution)/shard_map/while/body/eval_jaxpr/slice | solution.py:62
  650.6 5.0 fusion.46
  (248 shorter events, 321.2 us)
Async XLA Ops:
  0.6 6.3 copy-start.6
  6.9 10.3 %copy-start = (f32[72,4,4,1024]{3,2,1,0:T(4,128)S(1)}, f32[72,4,4,1024]{3,2,1,0:T(4,128)}, u32[]{:S(2)}) copy-start(f32[72,4,4,1024]{3,2,1,0:T(4,128)} %reshape.181) | copy-start | bytes 14155780
  6.9 10.4 %copy-start.13 = (f32[4,4]{0,1:T(4,128)S(1)}, f32[4,4]{0,1:T(4,128)}, u32[]{:S(2)}) copy-start(f32[4,4]{0,1:T(4,128)} %constant.182.clone) | copy-start | bytes 196
  30.8 4.9 copy-start.15
  35.7 3.1 copy-start.14
  39.5 8.9 %copy-start.7 = (s32[2,1024]{1,0:T(2,128)S(1)}, s32[2,1024]{1,0:T(2,128)}, u32[]{:S(2)}) copy-start(s32[2,1024]{1,0:T(2,128)} %param.23) | copy-start | bytes 24580
  39.5 8.9 %copy-start.11 = (f32[1024]{0:T(1024)S(1)}, f32[1024]{0:T(1024)}, u32[]{:S(2)}) copy-start(f32[1024]{0:T(1024)} %param.25) | copy-start | bytes 12292
  39.5 8.9 %copy-start.12 = (f32[1024]{0:T(1024)S(1)}, f32[1024]{0:T(1024)}, u32[]{:S(2)}) copy-start(f32[1024]{0:T(1024)} %param.26) | copy-start | bytes 12292
  39.5 8.9 %copy-start.10 = (s32[1024]{0:T(1024)S(1)}, s32[1024]{0:T(1024)}, u32[]{:S(2)}) copy-start(s32[1024]{0:T(1024)} %param.24) | copy-start | bytes 12292
  41.5 19.4 %collective-permute-start = (f32[73,8,512]{2,1,0:T(8,128)}, f32[73,8,512]{2,1,0:T(8,128)}, u32[]{:S(2)}, u32[]{:S(2)}) collective-permute-start(f32[73,8,512]{2,1,0:T(8,128)} %copy.46), channel_id=1, source_target_pairs={{0,1},{1,2},{2,3},{3,4},{4,5},{5,6},{6,7},{7,8},{8,9},{9,10},{10,1... | collective-permute-start | bytes 3588104 | tf_op jit(solution)/shard_map/ppermute | solution.py:20
  43.3 19.7 %collective-permute-start.1 = (f32[73,8,512]{2,1,0:T(8,128)}, f32[73,8,512]{2,1,0:T(8,128)}, u32[]{:S(2)}, u32[]{:S(2)}) collective-permute-start(f32[73,8,512]{2,1,0:T(8,128)} %copy.48), channel_id=1, source_target_pairs={{1,0},{2,1},{3,2},{4,3},{5,4},{6,5},{7,6},{8,7},{9,8},{10,9},{11,1... | collective-permute-start | bytes 3588104 | tf_op jit(solution)/shard_map/ppermute | solution.py:22
  63.0 5.4 copy-start.1
  120.4 5.2 copy-start.3
  120.4 5.2 copy-start.4
  120.4 5.2 copy-start.5
  125.7 530.0 %copy-start.8 = (pred[1024]{0:T(1024)(128)(4,1)S(1)}, pred[1024]{0:T(1024)(128)(4,1)}, u32[]{:S(2)}) copy-start(pred[1024]{0:T(1024)(128)(4,1)} %broadcast_compare_fusion) | copy-start | bytes 3076
  385.1 9.6 %slice-start = ((s8[16515072]{0:T(1024)(128)(4,1)}), s8[4194304]{0:T(1024)(128)(4,1)S(1)}, s32[]{:S(2)}) async-start(s8[16515072]{0:T(1024)(128)(4,1)} %bitcast.69), calls=%async_computation | async-start | bytes 8388608 | tf_op jit(solution)/shard_map/while
  385.1 9.6 %slice-start.1 = ((s8[16515072]{0:T(1024)(128)(4,1)}), s8[4194304]{0:T(1024)(128)(4,1)S(1)}, s32[]{:S(2)}) async-start(s8[16515072]{0:T(1024)(128)(4,1)} %bitcast.69), calls=%async_computation.1 | async-start | bytes 8388608 | tf_op jit(solution)/shard_map/while
  385.1 9.6 %slice-start.2 = ((s8[16515072]{0:T(1024)(128)(4,1)}), s8[4194304]{0:T(1024)(128)(4,1)S(1)}, s32[]{:S(2)}) async-start(s8[16515072]{0:T(1024)(128)(4,1)} %bitcast.69), calls=%async_computation.2 | async-start | bytes 8388608 | tf_op jit(solution)/shard_map/while
  385.1 10.6 %slice-start.3 = ((s8[16515072]{0:T(1024)(128)(4,1)}), s8[3932160]{0:T(1024)(128)(4,1)S(1)}, s32[]{:S(2)}) async-start(s8[16515072]{0:T(1024)(128)(4,1)} %bitcast.69), calls=%async_computation.3 | async-start | bytes 7864320 | tf_op jit(solution)/shard_map/while
  639.9 9.6 %slice-start = ((s8[16515072]{0:T(1024)(128)(4,1)}), s8[4194304]{0:T(1024)(128)(4,1)S(1)}, s32[]{:S(2)}) async-start(s8[16515072]{0:T(1024)(128)(4,1)} %bitcast.69), calls=%async_computation | async-start | bytes 8388608 | tf_op jit(solution)/shard_map/while
  639.9 9.6 %slice-start.1 = ((s8[16515072]{0:T(1024)(128)(4,1)}), s8[4194304]{0:T(1024)(128)(4,1)S(1)}, s32[]{:S(2)}) async-start(s8[16515072]{0:T(1024)(128)(4,1)} %bitcast.69), calls=%async_computation.1 | async-start | bytes 8388608 | tf_op jit(solution)/shard_map/while
  639.9 9.6 %slice-start.2 = ((s8[16515072]{0:T(1024)(128)(4,1)}), s8[4194304]{0:T(1024)(128)(4,1)S(1)}, s32[]{:S(2)}) async-start(s8[16515072]{0:T(1024)(128)(4,1)} %bitcast.69), calls=%async_computation.2 | async-start | bytes 8388608 | tf_op jit(solution)/shard_map/while
  639.9 10.6 %slice-start.3 = ((s8[16515072]{0:T(1024)(128)(4,1)}), s8[3932160]{0:T(1024)(128)(4,1)S(1)}, s32[]{:S(2)}) async-start(s8[16515072]{0:T(1024)(128)(4,1)} %bitcast.69), calls=%async_computation.3 | async-start | bytes 7864320 | tf_op jit(solution)/shard_map/while
  (2 other events, 4.1 us)
where the time goes:
time: 669 us; the launch traced here: 657 us
  other arithmetic  500 us (75%)
  local copies, waits for them, and re-layouts  99.4 us (15%)
  matrix products  23.8 us (4%)
  loops' own time  20.6 us (3%)
    dynamic_update_slice x144, other arithmetic, radiate(): lax.scan(climb_up, start_albedo, (reflect, diffuse), reverse=True)  272 us
    another operation x2, other arithmetic, radiate(): column_depth = jnp.cumsum(layer_tau, axis=0)  166 us
    exp x2, other arithmetic, radiate(): diffuse = jnp.exp(-DIFFUSE_FACTOR * layer_tau)  24.5 us
    another operation x1, loops' own time, radiate_blocks(): lax.map(one_block, (q_blocks, cos_zenith.reshape(block_count, block_size)...  20.5 us
    another operation x2, local copies, waits for them, and re-layouts  15.5 us
    slice x2, local copies, waits for them, and re-layouts, radiate(): net_next = jnp.concatenate([net_top[1:], net_bottom[None]], axis=0)  15.4 us
    dot_general x1, matrix products, shards(): jnp.einsum('ik,lkjn->lijn', second_diff, nodal, precision=highest)  13.5 us
  transfers between devices with their start and end apart: 2, of which 1 were waited for; matrix products, arithmetic and copies ran while one was open for 2% of the time, Pallas kernels for 0%

commit v1 on v0

v1 whole, which is shorter than its diff:
```python
import numpy as np
import jax
import jax.numpy as jnp
from jax import lax
from jax.experimental import pallas as pl
from jax.experimental.pallas import tpu as pltpu
from jax.sharding import PartitionSpec as P

LEV, G, E = 72, 112, 1024
HALF, LANES, GROUPS = E // 2, 128, LEV // 8
ROOT5 = float(np.sqrt(5.0))
STEP_SIZE = 0.02
CROSSED = (1, 2, 13, 14)
WEST, EAST = (4, 8), (7, 11)
J_ROW, PACK_ROW, SEND_ROWS = 288, 296, 304
G_BLOCKS = G // 8
EXPONENT = -1.66 * 1.4426950408889634


def second(v):
    mean = 1.25 * ((v[0] + v[3]) - (v[1] + v[2]))
    slope = 3.75 * ((v[0] - v[3]) - ROOT5 * (v[1] - v[2]))
    inner = slope * (1.0 / ROOT5)
    return (mean + slope, mean + inner, mean - inner, mean - slope)


def edge_values(m_ref, head_in, head_ref, tail_ref, tiles):
    group = pl.program_id(0)
    lane = lax.broadcasted_iota(jnp.int32, (8, LANES), 1)

    @pl.when(group == 0)
    def _():
        head_ref[J_ROW:J_ROW + 8] = jnp.broadcast_to(head_in[:, :HALF], (8, HALF))
        tail_ref[J_ROW:J_ROW + 8] = jnp.broadcast_to(head_in[:, HALF:], (8, HALF))
        head_ref[PACK_ROW:PACK_ROW + 8] = jnp.zeros((8, HALF), jnp.float32)
        tail_ref[PACK_ROW:PACK_ROW + 8] = jnp.zeros((8, HALF), jnp.float32)

    for block in range(E // LANES):
        cols = pl.ds(block * LANES, LANES)
        tiles[...] = m_ref[:, cols]
        node = {n: tiles[pl.ds(n, 8, stride=16), :] for n in range(16)}
        x_one = second([node[4 * k + 1] for k in range(4)])
        x_two = second([node[4 * k + 2] for k in range(4)])
        y_first = second([node[k] for k in range(4)])
        y_last = second([node[12 + k] for k in range(4)])
        values = (x_one[0] + y_first[1], x_two[0] + y_first[2], x_one[3] + y_last[1], x_two[3] + y_last[2])
        side, offset = (head_ref, block * LANES) if block * LANES < HALF else (tail_ref, block * LANES - HALF)
        for c, value in enumerate(values):
            rows = pl.ds(pl.multiple_of(c * LEV + group * 8, 8), 8)
            side[rows, pl.ds(offset, LANES)] = value
        for side, at, nodes, column, place in ((head_ref, 0, 0, 0, 0), (tail_ref, E // LANES - 1, 3, LANES - 1, 0)):
            if block != at:
                continue
            x_side = second([node[4 * k + nodes] for k in range(4)])
            y_one = second([node[4 + k] for k in range(4)])
            y_two = second([node[8 + k] for k in range(4)])
            packed = side[PACK_ROW:PACK_ROW + 8, :LANES]
            for a, value in enumerate((x_side[1] + y_one[nodes], x_side[2] + y_two[nodes])):
                spread = jnp.broadcast_to(value[:, column:column + 1], (8, LANES))
                packed = jnp.where(lane == a * GROUPS + group, spread, packed)
            side[PACK_ROW:PACK_ROW + 8, :LANES] = packed


def take_lanes(source, index):
    return jnp.take_along_axis(source, index, axis=1)


def assemble(m_ref, j_ref, partner_ref, head, tail, before, after, new_ref, q_ref, edge, scale, tiles, made):
    group = pl.program_id(0)
    lane = lax.broadcasted_iota(jnp.int32, (8, LANES), 1)
    blocks = E // LANES

    def crossing(side, rows_at, block):
        first, second_half = (before, head) if block < blocks // 2 else (tail, after)
        index = (partner_ref[side:side + 1, pl.ds(block * LANES, LANES)] + HALF) & (E - 1)
        index = jnp.broadcast_to(index, (8, LANES))
        inside, slot = index & (LANES - 1), index >> 7
        results = [None] * len(rows_at)
        for k in range(blocks):
            source = first if k < blocks // 2 else second_half
            here = slot == k
            for r, start in enumerate(rows_at):
                part = take_lanes(source[pl.ds(start, 8), pl.ds((k % (blocks // 2)) * LANES, LANES)], inside)
                results[r] = part if k == 0 else jnp.where(here, part, results[r])
        return results

    @pl.when(group == 0)
    def _():
        j_own = jnp.broadcast_to(j_ref[...], (8, E))
        for block in range(blocks):
            cols = pl.ds(block * LANES, LANES)
            own = j_own[:, block * LANES:(block + 1) * LANES]
            left = before[J_ROW:J_ROW + 8, HALF - LANES:] if block == 0 else j_own[:, (block - 1) * LANES:block * LANES]
            right = after[J_ROW:J_ROW + 8, :LANES] if block == blocks - 1 else j_own[:, (block + 1) * LANES:(block + 2) * LANES]
            west = jnp.where(lane == 0, pltpu.roll(left, 1, 1), pltpu.roll(own, 1, 1))
            east = jnp.where(lane == LANES - 1, pltpu.roll(right, LANES - 1, 1), pltpu.roll(own, LANES - 1, 1))
            south, = crossing(0, (J_ROW,), block)
            north, = crossing(1, (J_ROW,), block)
            scale[0, :, cols] = STEP_SIZE / own
            for s, other in enumerate((west, east, south, north)):
                scale[1 + s, :, cols] = STEP_SIZE / (own + other)

    for block in range(blocks):
        cols = pl.ds(block * LANES, LANES)
        tiles[block] = m_ref[:, cols]
        node = [tiles[block, pl.ds(n, 8, stride=16), :] for n in range(16)]
        along_x = [second([node[4 * k + j] for k in range(4)]) for j in range(4)]
        along_y = [second([node[4 * i + k] for k in range(4)]) for i in range(4)]
        inverse = scale[0, :, cols]
        corner, inner = 0.0, 0.0
        for n in range(16):
            i, j = n // 4, n % 4
            value = along_x[j][i] + along_y[i][j]
            ends = (i in (0, 3)) + (j in (0, 3))
            if ends == 1:
                edge[(WEST + EAST + CROSSED).index(n), :, cols] = value
                continue
            new = node[n] + inverse * value
            made[block, pl.ds(n, 8, stride=16), :] = new
            if ends == 2:
                corner = corner + new
            else:
                inner = inner + new
        q_ref[:, cols] = corner * (1.0 / 144.0) + inner * (25.0 / 144.0)

    packs = [
        [take_lanes(side[PACK_ROW:PACK_ROW + 8, :LANES], jnp.zeros((8, LANES), jnp.int32) + (a * GROUPS + group)) for a in range(2)]
        for side in (before, after)
    ]
    starts = [pl.multiple_of(c * LEV + group * 8, 8) for c in range(4)]
    for block in range(blocks):
        cols = pl.ds(block * LANES, LANES)
        others = []
        for a in range(2):
            own = edge[2 + a, :, cols]
            carried = packs[0][a] if block == 0 else pltpu.roll(edge[2 + a, :, pl.ds((block - 1) * LANES, LANES)], 1, 1)
            others.append(jnp.where(lane == 0, carried, pltpu.roll(own, 1, 1)))
        for a in range(2):
            own = edge[a, :, cols]
            if block == blocks - 1:
                carried = packs[1][a]
            else:
                carried = pltpu.roll(edge[a, :, pl.ds((block + 1) * LANES, LANES)], LANES - 1, 1)
            others.append(jnp.where(lane == LANES - 1, carried, pltpu.roll(own, LANES - 1, 1)))
        others += crossing(0, (starts[1], starts[0]), block)
        others += crossing(1, (starts[3], starts[2]), block)
        total = 0.0
        for k, n in enumerate(WEST + EAST + CROSSED):
            value = edge[k, :, cols] + others[k]
            new = tiles[block, pl.ds(n, 8, stride=16), :] + scale[1 + k // 2, :, cols] * value
            made[block, pl.ds(n, 8, stride=16), :] = new
            total = total + new
        q_ref[:, cols] += total * (5.0 / 144.0)
        new_ref[:, cols] = made[block]


def radiate(q_ref, mu_ref, alb_ref, lit_ref, absorb_ref, ray_ref, solar_ref, out_ref, absb, rayb, solb, flux, partial, q_wide):
    scaled = absorb_ref[...] * EXPONENT
    for level in range(LEV):
        absb[level] = jnp.broadcast_to(scaled[:, level:level + 1], (G, LANES)).reshape(G_BLOCKS, 8, LANES)
    rayb[...] = jnp.broadcast_to(ray_ref[...] * EXPONENT, (G, LANES)).reshape(G_BLOCKS, 8, LANES)
    solb[...] = jnp.broadcast_to(solar_ref[...], (G, LANES)).reshape(G_BLOCKS, 8, LANES)

    def one_block(block, carry):
        cols = pl.ds(pl.multiple_of(block * LANES, LANES), LANES)
        lit = lit_ref[0:1, cols]
        count = jnp.sum(lit)

        @pl.when(count == 0)
        def _():
            out_ref[:, cols] = jnp.zeros((LEV, LANES), jnp.float32)

        @pl.when(count > 0)
        def _():
            mu = mu_ref[0:1, cols]
            alb = alb_ref[0:1, cols]
            slant = jnp.broadcast_to(1.0 / (1.66 * mu), (8, LANES))
            square = q_ref[:, cols]
            square = square * square
            for level in range(LEV):
                q_wide[level] = jnp.broadcast_to(square[level:level + 1], (8, LANES))

            def down(level, direct):
                flux[level] = direct
                depth = absb[level] * q_wide[level][None] + rayb[...]
                return direct * jnp.exp2(depth * slant[None])

            direct = lax.fori_loop(0, LEV, down, solb[...], unroll=4)
            partial[LEV] = jnp.sum(direct * (1.0 - alb)[None], axis=0)

            def up(step, below):
                level = LEV - 1 - step
                ray = rayb[...]
                depth = absb[level] * q_wide[level][None] + ray
                diffuse = jnp.exp2(depth)
                half = ray * 0.5
                rho = half - half * diffuse
                rest = depth - rho * below
                through = diffuse * depth
                above = (rho * rest + through * through * below) / (depth * rest)
                partial[level] = jnp.sum(flux[level] * (1.0 - above), axis=0)
                return above

            lax.fori_loop(0, LEV, up, jnp.broadcast_to(alb[None], (G_BLOCKS, 8, LANES)), unroll=4)
            net = jnp.sum(partial[...], axis=1)
            heat = (net[:LEV] - net[1:LEV + 1]) * (72.0 * mu)
            out_ref[:, cols] = jnp.where(lit == 1, heat, 0.0)

        return carry

    lax.fori_loop(0, E // LANES, one_block, 0)


def whole(shape):
    return pl.BlockSpec(shape, lambda g: (0,) * len(shape))


def shards(moisture, jacobian, partners, daylit, cos_zenith, albedo, absorb, rayleigh, solar):
    f32 = jnp.float32
    flat = moisture.reshape(LEV * 16, E)
    jac = jacobian.reshape(1, E)
    rows = pl.BlockSpec((128, E), lambda g: (g, 0))
    head, tail = pl.pallas_call(
        edge_values,
        grid=(GROUPS,),
        in_specs=[rows, whole((1, E))],
        out_specs=[whole((SEND_ROWS, HALF))] * 2,
        out_shape=[jax.ShapeDtypeStruct((SEND_ROWS, HALF), f32)] * 2,
        scratch_shapes=[pltpu.VMEM((128, LANES), f32)],
        name="edge_values",
    )(flat, jac)
    count = lax.axis_size("curve")
    before = lax.ppermute(tail, "curve", [(i, (i + 1) % count) for i in range(count)])
    after = lax.ppermute(head, "curve", [((i + 1) % count, i) for i in range(count)])
    new, column_q = pl.pallas_call(
        assemble,
        grid=(GROUPS,),
        in_specs=[rows, whole((1, E)), whole((2, E))] + [whole((SEND_ROWS, HALF))] * 4,
        out_specs=[rows, pl.BlockSpec((8, E), lambda g: (g, 0))],
        out_shape=[jax.ShapeDtypeStruct((LEV * 16, E), f32), jax.ShapeDtypeStruct((LEV, E), f32)],
        scratch_shapes=[
            pltpu.VMEM((8, 8, E), f32),
            pltpu.VMEM((5, 8, E), f32),
            pltpu.VMEM((8, 128, LANES), f32),
            pltpu.VMEM((8, 128, LANES), f32),
        ],
        name="assemble",
    )(flat, jac, partners, head, tail, before, after)
    heating = pl.pallas_call(
        radiate,
        in_specs=[pl.BlockSpec(memory_space=pltpu.VMEM)] * 7,
        out_specs=pl.BlockSpec(memory_space=pltpu.VMEM),
        out_shape=jax.ShapeDtypeStruct((LEV, E), f32),
        scratch_shapes=[
            pltpu.VMEM((LEV, G_BLOCKS, 8, LANES), f32),
            pltpu.VMEM((G_BLOCKS, 8, LANES), f32),
            pltpu.VMEM((G_BLOCKS, 8, LANES), f32),
            pltpu.VMEM((LEV, G_BLOCKS, 8, LANES), f32),
            pltpu.VMEM((LEV + 1, 8, LANES), f32),
            pltpu.VMEM((LEV, 8, LANES), f32),
        ],
        compiler_params=pltpu.CompilerParams(vmem_limit_bytes=48 * 2**20),
        name="radiate",
    )(
        column_q,
        cos_zenith.reshape(1, E),
        albedo.reshape(1, E),
        daylit.reshape(1, E),
        absorb,
        rayleigh.reshape(G, 1),
        solar.reshape(G, 1),
    )
    return (new.reshape(LEV, 16, E), heating)


def solution(mesh):
    columns = P(("group", "curve"))
    placed = (
        P(None, None, ("group", "curve")),
        columns,
        P(None, ("group", "curve")),
        columns,
        columns,
        columns,
        P(),
        P(),
        P(),
    )
    return jax.shard_map(
        shards,
        mesh=mesh,
        in_specs=placed,
        out_specs=(P(None, None, ("group", "curve")), P(None, ("group", "curve"))),
        check_vma=False,
    )
```

time: 669 us -> 71.5 us (0.11); the launches traced: 657 us -> 71 us
  other arithmetic: 500 us -> 0 us
  local copies, waits for them, and re-layouts: 99.4 us -> 2.96 us
  Pallas kernels: 0 us -> 54.4 us
  matrix products: 23.8 us -> 0 us
  loops' own time: 20.6 us -> 0 us
    dynamic_update_slice x146 -> x0, other arithmetic: 272 us -> none  [the longest x144 272 us: radiate(): lax.scan(climb_up, start_albedo, (reflect, diffuse), reverse=True)]
    another operation x2 -> x0, other arithmetic: 166 us -> none  [radiate(): column_depth = jnp.cumsum(layer_tau, axis=0)]
    pallas_call x0 -> x3, Pallas kernels: none -> 54.4 us  [the longest x1 34.8 us: shards(): pl.pallas_call(radiate, in_specs=[pl.BlockSpec(memory_space=pltpu.VMEM)]...]
    slice x8 -> x0, local copies, waits for them, and re-layouts: 27.3 us -> none  [the longest x2 15.4 us: radiate(): net_next = jnp.concatenate([net_top[1:], net_bottom[None]], axis=0)]
    gather x6 -> x0, local copies, waits for them, and re-layouts: 25.4 us -> none  [the longest x2 11.3 us: shards(): north_side = jnp.take(crossed[:, 2:4], rel_index[1], axis=2)[:, ::-1]]
    exp x2 -> x0, other arithmetic: 24.5 us -> none  [radiate(): diffuse = jnp.exp(-DIFFUSE_FACTOR * layer_tau)]
    dot_general x2 -> x0, matrix products: 23.8 us -> none  [the longest x1 13.5 us: shards(): jnp.einsum('ik,lkjn->lijn', second_diff, nodal, precision=highest)]
    another operation x3 -> x0, loops' own time: 20.6 us -> none  [the longest x1 20.5 us: radiate_blocks(): lax.map(one_block, (q_blocks, cos_zenith.reshape(block_count, block_size)...]
  transfers between devices with their start and end apart: 2 -> 2, of which waited for: 1 -> 1; matrix products, arithmetic and copies ran while one was open for 2% -> 0% of each run, Pallas kernels for 0% -> 0%
where the time goes in v1:
time: 71.5 us; the launch traced here: 71 us
  Pallas kernels  54.4 us (76%)
  waiting for transfers between devices  7.8 us (11%)
  starting transfers between devices  5.13 us (7%)
  local copies, waits for them, and re-layouts  2.96 us (4%)
  between operations  0.72 us (1%)
    pallas_call x1, Pallas kernels, shards(): pl.pallas_call(radiate, in_specs=[pl.BlockSpec(memory_space=pltpu.VMEM)]...  34.8 us
    pallas_call x1, Pallas kernels, shards(): pl.pallas_call(assemble, grid=(GROUPS,), in_specs=[rows, whole((1, E)), w...  11.7 us
    pallas_call x1, Pallas kernels, shards(): pl.pallas_call(edge_values, grid=(GROUPS,), in_specs=[rows, whole((1, E))...  7.86 us
    ppermute x1, waiting for transfers between devices, shards(): lax.ppermute(tail, 'curve', [(i, (i + 1) % count) for i in range(count)])  7.8 us
    ppermute x1, starting transfers between devices, shards(): lax.ppermute(head, 'curve', [((i + 1) % count, i) for i in range(count)])  5.05 us
    unnamed x19, local copies, waits for them, and re-layouts  2.75 us
  transfers between devices with their start and end apart: 2, of which 1 were waited for; matrix products, arithmetic and copies ran while one was open for 0% of the time, Pallas kernels for 0%

profile of v1, /device:TPU:0, one launch (start us, length us, event | category | flops | bytes accessed | tf_op | source)
XLA Modules:
  0.0 71.0 jit_solution(2102382872541001704)
XLA Ops:
  0.6 0.0 copy-start.6
  0.6 0.0 copy-start.7
  0.7 0.0 copy-start.8
  0.7 7.9 %edge_values.1 = (f32[304,512]{1,0:T(8,128)}, f32[304,512]{1,0:T(8,128)}) custom-call(f32[1152,1024]{1,0:T(8,128)} %bitcast.11, f32[1,1024]{1,0:T(1,128)} %bitcast.13), custom_call_target="tpu_custom_call" | custom-call | tf_op jit(solution)/shard_map/edge_values/pallas_call | solution.py:223
  8.5 0.0 copy-start.1
  8.5 0.1 collective-permute-start
  8.6 5.1 %collective-permute-start.1 = (f32[304,512]{1,0:T(8,128)}, f32[304,512]{1,0:T(8,128)S(1)}, u32[]{:S(2)}, u32[]{:S(2)}) collective-permute-start(f32[304,512]{1,0:T(8,128)} %get-tuple-element.6.head), channel_id=1, source_target_pairs={{1,0},{2,1},{3,2},{4,3},{5,4},{6,5},{7,6},{8,7},{9,8},{10,9},{11,1... | collective-permute-start | bytes 1867784 | tf_op jit(solution)/shard_map/ppermute | solution.py:234
  13.7 0.0 copy-done.6
  13.7 0.1 copy.11.absorb_ref
  13.8 0.0 copy-done.7
  13.8 0.1 copy.12.ray_ref
  13.9 0.0 copy-done.8
  13.9 0.1 copy.13.solar_ref
  14.0 7.8 %collective-permute-done.before = f32[304,512]{1,0:T(8,128)S(1)} collective-permute-done((f32[304,512]{1,0:T(8,128)}, f32[304,512]{1,0:T(8,128)S(1)}, u32[]{:S(2)}, u32[]{:S(2)}) %collective-permute-start) | collective-permute-done | bytes 622624 | tf_op jit(solution)/shard_map/ppermute | solution.py:233
  21.8 0.0 collective-permute-done.1.after
  21.8 0.9 %copy-done.4 = f32[304,512]{1,0:T(8,128)} copy-done((f32[304,512]{1,0:T(8,128)}, f32[304,512]{1,0:T(8,128)S(1)}, u32[]{:S(2)}) %copy-start.4) | copy-done | bytes 622616
  22.7 0.8 %copy-done.5 = f32[304,512]{1,0:T(8,128)} copy-done((f32[304,512]{1,0:T(8,128)}, f32[304,512]{1,0:T(8,128)S(1)}, u32[]{:S(2)}) %copy-start.5) | copy-done | bytes 622616
  23.5 11.7 %assemble.1 = (f32[1152,1024]{1,0:T(8,128)}, f32[72,1024]{1,0:T(8,128)}) custom-call(f32[1152,1024]{1,0:T(8,128)} %bitcast.12, f32[1,1024]{1,0:T(1,128)} %bitcast.14, s32[2,1024]{1,0:T(2,128)} %partner_ref.1, f32[304,512]{1,0:T(8,128)} %get-tuple-element.6.head, f32[304,512]{1,0:T(8,128)} %get-tuple-element.7.tail, f32[304,512]{1,0:T(8,128)} %copy-done.4, ...), custom_call_target="tpu_custom_call" | custom-call | tf_op jit(solution)/shard_map/assemble/pallas_call | solution.py:235
  35.2 0.0 copy-done.1
  35.2 0.0 copy-done.2
  35.2 0.0 copy-done.3
  35.2 0.0 copy-start
  35.2 1.0 %copy-done = f32[72,1024]{1,0:T(8,128)S(1)} copy-done((f32[72,1024]{1,0:T(8,128)S(1)}, f32[72,1024]{1,0:T(8,128)}, u32[]{:S(2)}) %copy-start) | copy-done | bytes 294936
  36.2 34.8 %radiate.1 = f32[72,1024]{1,0:T(8,128)} custom-call(f32[72,1024]{1,0:T(8,128)S(1)} %copy-done, f32[1,1024]{1,0:T(1,128)S(1)} %bitcast.8, f32[1,1024]{1,0:T(1,128)S(1)} %bitcast.9, s32[1,1024]{1,0:T(1,128)S(1)} %bitcast.10, f32[112,72]{1,0:T(8,128)S(1)} %copy.11.absorb_ref, f32[112,1]{1,0:T(8,128)S(1)} %copy.12.ray_ref, f32[112,1]{1,0:T(8,128)S(1)} %copy.13.solar_ref), custom_call_target="tpu_custom_call" | custom-call | tf_op jit(solution)/shard_map/radiate/pallas_call | solution.py:249
  (4 shorter events, 0.0 us)
Async XLA Ops:
  0.6 13.0 %copy-start.6 = (f32[112,72]{0,1:T(8,128)S(1)}, f32[112,72]{0,1:T(8,128)}, u32[]{:S(2)}) copy-start(f32[112,72]{0,1:T(8,128)} %param.15) | copy-start | bytes 96772
  0.6 13.1 %copy-start.7 = (f32[112]{0:T(128)S(1)}, f32[112]{0:T(128)}, u32[]{:S(2)}) copy-start(f32[112]{0:T(128)} %param.16) | copy-start | bytes 1348
  0.7 13.2 %copy-start.8 = (f32[112]{0:T(128)S(1)}, f32[112]{0:T(128)}, u32[]{:S(2)}) copy-start(f32[112]{0:T(128)} %param.17) | copy-start | bytes 1348
  8.5 26.7 %copy-start.1 = (f32[1024]{0:T(1024)S(1)}, f32[1024]{0:T(1024)}, u32[]{:S(2)}) copy-start(f32[1024]{0:T(1024)} %param.13) | copy-start | bytes 12292
  8.5 26.7 %copy-start.2 = (f32[1024]{0:T(1024)S(1)}, f32[1024]{0:T(1024)}, u32[]{:S(2)}) copy-start(f32[1024]{0:T(1024)} %param.14) | copy-start | bytes 12292
  8.5 26.7 %copy-start.3 = (s32[1024]{0:T(1024)S(1)}, s32[1024]{0:T(1024)}, u32[]{:S(2)}) copy-start(s32[1024]{0:T(1024)} %param.12) | copy-start | bytes 12292
  8.5 13.3 %collective-permute-start = (f32[304,512]{1,0:T(8,128)}, f32[304,512]{1,0:T(8,128)S(1)}, u32[]{:S(2)}, u32[]{:S(2)}) collective-permute-start(f32[304,512]{1,0:T(8,128)} %get-tuple-element.7.tail), channel_id=1, source_target_pairs={{0,1},{1,2},{2,3},{3,4},{4,5},{5,6},{6,7},{7,8},{8,9},{9,10},{10,1... | collective-permute-start | bytes 1867784 | tf_op jit(solution)/shard_map/ppermute | solution.py:233
  8.6 13.2 %collective-permute-start.1 = (f32[304,512]{1,0:T(8,128)}, f32[304,512]{1,0:T(8,128)S(1)}, u32[]{:S(2)}, u32[]{:S(2)}) collective-permute-start(f32[304,512]{1,0:T(8,128)} %get-tuple-element.6.head), channel_id=1, source_target_pairs={{1,0},{2,1},{3,2},{4,3},{5,4},{6,5},{7,6},{8,7},{9,8},{10,9},{11,1... | collective-permute-start | bytes 1867784 | tf_op jit(solution)/shard_map/ppermute | solution.py:234
  21.8 0.9 %copy-start.4 = (f32[304,512]{1,0:T(8,128)}, f32[304,512]{1,0:T(8,128)S(1)}, u32[]{:S(2)}) copy-start(f32[304,512]{1,0:T(8,128)S(1)} %collective-permute-done.before) | copy-start | bytes 1867780
  22.7 0.8 %copy-start.5 = (f32[304,512]{1,0:T(8,128)}, f32[304,512]{1,0:T(8,128)S(1)}, u32[]{:S(2)}) copy-start(f32[304,512]{1,0:T(8,128)S(1)} %collective-permute-done.1.after) | copy-start | bytes 1867780
  35.2 1.0 %copy-start = (f32[72,1024]{1,0:T(8,128)S(1)}, f32[72,1024]{1,0:T(8,128)}, u32[]{:S(2)}) copy-start(f32[72,1024]{1,0:T(8,128)} %get-tuple-element.9.q_ref) | copy-start | bytes 884740

commit v2 on v1

v2 whole, which is shorter than its diff:
```python
import numpy as np
import jax
import jax.numpy as jnp
from jax import lax
from jax.experimental import pallas as pl
from jax.experimental.pallas import tpu as pltpu
from jax.sharding import PartitionSpec as P

LEV, G, E = 72, 112, 1024
HALF, LANES, GROUPS = E // 2, 128, LEV // 8
ROOT5 = float(np.sqrt(5.0))
STEP_SIZE = 0.02
CROSSED = (1, 2, 13, 14)
SIDES = (4, 8, 7, 11)
G_BLOCKS = G // 8
EXPONENT = -1.66 * 1.4426950408889634


def second(v):
    mean = 1.25 * ((v[0] + v[3]) - (v[1] + v[2]))
    slope = 3.75 * ((v[0] - v[3]) - ROOT5 * (v[1] - v[2]))
    inner = slope * (1.0 / ROOT5)
    return (mean + slope, mean + inner, mean - inner, mean - slope)


def take_lanes(source, index):
    return jnp.take_along_axis(source, index, axis=1)


def exchange(
    m_hbm, j_hbm, partner_hbm, new_hbm, q_ref, held, made, sides, crossed, jac, scale, inside, slot,
    j_ref, partner_ref, in_sem, out_sem, send_sem, recv_sem,
):
    me = lax.axis_index("curve")
    count = lax.axis_size("curve")
    right, left = lax.rem(me + 1, count), lax.rem(me + count - 1, count)
    blocks = E // LANES
    lane = lax.broadcasted_iota(jnp.int32, (8, LANES), 1)

    def fetch(group):
        rows = pl.ds(pl.multiple_of(group * 128, 128), 128)
        return pltpu.make_async_copy(m_hbm.at[rows], held.at[group], in_sem.at[group])

    def deliver(group):
        rows = pl.ds(pl.multiple_of(group * 128, 128), 128)
        return pltpu.make_async_copy(held.at[group], new_hbm.at[rows], out_sem.at[group])

    def send(way, group):
        return pltpu.make_async_remote_copy(
            src_ref=crossed.at[group, 2 - way],
            dst_ref=crossed.at[group, 3 * way],
            send_sem=send_sem.at[way, group],
            recv_sem=recv_sem.at[way, group],
            device_id={"curve": left if way else right},
            device_id_type=pl.DeviceIdType.MESH,
        )

    def send_jacobian(way):
        return pltpu.make_async_remote_copy(
            src_ref=jac.at[pl.ds(4 if way else 8, 4)],
            dst_ref=jac.at[pl.ds(12 if way else 0, 4)],
            send_sem=send_sem.at[way, GROUPS],
            recv_sem=recv_sem.at[way, GROUPS],
            device_id={"curve": left if way else right},
            device_id_type=pl.DeviceIdType.MESH,
        )

    barrier = pltpu.get_barrier_semaphore()
    for neighbour in (left, right):
        pl.semaphore_signal(barrier, inc=1, device_id={"curve": neighbour}, device_id_type=pl.DeviceIdType.MESH)
    small = [
        pltpu.make_async_copy(j_hbm, j_ref, in_sem.at[GROUPS]),
        pltpu.make_async_copy(partner_hbm, partner_ref, in_sem.at[GROUPS + 1]),
    ]
    for copy in small:
        copy.start()
    for group in range(GROUPS):
        fetch(group).start()
    for copy in small:
        copy.wait()
    for block in range(blocks):
        cols = pl.ds(block * LANES, LANES)
        own = jnp.broadcast_to(j_ref[:, cols], (8, LANES))
        jac[4 + block] = own
        scale[0, block] = STEP_SIZE / own
        for side in range(2):
            index = (jnp.broadcast_to(partner_ref[side:side + 1, cols], (8, LANES)) + HALF) & (E - 1)
            inside[side, block] = index & (LANES - 1)
            slot[side, block] = index >> 7
    pl.semaphore_wait(barrier, 2)
    for way in range(2):
        send_jacobian(way).start()

    def first_part(group, carry):
        fetch(group).wait()
        for block in range(blocks):
            cols = pl.ds(block * LANES, LANES)
            made[group, block] = held[group, :, cols]
            node = [made[group, block, pl.ds(n, 8, stride=16), :] for n in range(16)]
            along_x = [second([node[4 * k + j] for k in range(4)]) for j in range(4)]
            along_y = [second([node[4 * i + k] for k in range(4)]) for i in range(4)]
            inverse = scale[0, block]
            corner, inner = 0.0, 0.0
            section, place = 1 + block // 4, (block % 4) * 4
            for n in range(16):
                i, j = n // 4, n % 4
                value = along_x[j][i] + along_y[i][j]
                if n in CROSSED:
                    crossed[group, section, place + CROSSED.index(n)] = value
                    continue
                if n in SIDES:
                    k = SIDES.index(n)
                    sides[group, k, block] = value
                    if block == 0 and k < 2:
                        crossed[group, 1, 16 + k] = value
                    if block == blocks - 1 and k >= 2:
                        crossed[group, 2, 16 + k - 2] = value
                    continue
                new = node[n] + inverse * value
                made[group, block, pl.ds(n, 8, stride=16), :] = new
                if i in (0, 3):
                    corner = corner + new
                else:
                    inner = inner + new
            q_ref[pl.ds(pl.multiple_of(group * 8, 8), 8), cols] = corner * (1.0 / 144.0) + inner * (25.0 / 144.0)
        for way in range(2):
            send(way, group).start()
        return carry

    lax.fori_loop(0, GROUPS, first_part, 0)

    def gather(side, block, window):
        where, which = inside[side, block], slot[side, block]
        results = None
        for k in range(blocks):
            parts = [take_lanes(source, where) for source in window(k)]
            here = which == k
            results = parts if k == 0 else [jnp.where(here, p, r) for p, r in zip(parts, results)]
        return results

    for way in range(2):
        send_jacobian(way).wait()
    for block in range(blocks):
        own = jac[4 + block]
        west = jnp.where(lane == 0, pltpu.roll(jac[3 + block], 1, 1), pltpu.roll(own, 1, 1))
        east = jnp.where(lane == LANES - 1, pltpu.roll(jac[5 + block], LANES - 1, 1), pltpu.roll(own, LANES - 1, 1))
        base = 8 * (block // 4)
        south, = gather(0, block, lambda k: [jac[base + k]])
        north, = gather(1, block, lambda k: [jac[base + k]])
        for s, other in enumerate((west, east, south, north)):
            scale[1 + s, block] = STEP_SIZE / (own + other)

    def second_part(group, carry):
        for way in range(2):
            send(way, group).wait()
        for block in range(blocks):
            cols = pl.ds(block * LANES, LANES)
            section, place = 1 + block // 4, (block % 4) * 4
            others = []
            for a in range(2):
                last = crossed[group, 0, 16 + a] if block == 0 else sides[group, 2 + a, block - 1]
                others.append(jnp.where(lane == 0, pltpu.roll(last, 1, 1), pltpu.roll(sides[group, 2 + a, block], 1, 1)))
            for a in range(2):
                following = crossed[group, 3, 16 + a] if block == blocks - 1 else sides[group, a, block + 1]
                others.append(
                    jnp.where(lane == LANES - 1, pltpu.roll(following, LANES - 1, 1), pltpu.roll(sides[group, a, block], LANES - 1, 1))
                )
            for side in range(2):
                def window(k):
                    return [crossed[group, 2 * (block // 4) + k // 4, (k % 4) * 4 + 2 * side + c] for c in (1, 0)]
                others += gather(side, block, window)
            total = 0.0
            for k, n in enumerate(SIDES + CROSSED):
                own = sides[group, k, block] if k < 4 else crossed[group, section, place + k - 4]
                new = made[group, block, pl.ds(n, 8, stride=16), :] + scale[1 + k // 2, block] * (own + others[k])
                made[group, block, pl.ds(n, 8, stride=16), :] = new
                total = total + new
            q_ref[pl.ds(pl.multiple_of(group * 8, 8), 8), cols] += total * (5.0 / 144.0)
            held[group, :, cols] = made[group, block]
        deliver(group).start()
        return carry

    lax.fori_loop(0, GROUPS, second_part, 0)

    def finish(group, carry):
        deliver(group).wait()
        return carry

    lax.fori_loop(0, GROUPS, finish, 0)


def radiate(q_hbm, mu_ref, alb_ref, lit_ref, absorb_ref, ray_ref, solar_ref, new_ref, out_ref, kept_ref, absb, rayb, solb, flux, partial, q_wide, q_ref, kept_sem, q_sem):
    fetch = pltpu.make_async_copy(q_hbm, q_ref, q_sem)
    fetch.start()
    keep = pltpu.make_async_copy(new_ref, kept_ref, kept_sem)
    keep.start()
    scaled = absorb_ref[...].T * EXPONENT
    for level in range(LEV):
        absb[level] = jnp.broadcast_to(scaled[:, level:level + 1], (G, LANES)).reshape(G_BLOCKS, 8, LANES)
    rayb[...] = jnp.broadcast_to(ray_ref[...].T * EXPONENT, (G, LANES)).reshape(G_BLOCKS, 8, LANES)
    solb[...] = jnp.broadcast_to(solar_ref[...].T, (G, LANES)).reshape(G_BLOCKS, 8, LANES)

    fetch.wait()

    def one_block(block, carry):
        cols = pl.ds(pl.multiple_of(block * LANES, LANES), LANES)
        lit = lit_ref[0:1, cols]
        count = jnp.sum(lit)

        @pl.when(count == 0)
        def _():
            out_ref[:, cols] = jnp.zeros((LEV, LANES), jnp.float32)

        @pl.when(count > 0)
        def _():
            mu = mu_ref[0:1, cols]
            alb = alb_ref[0:1, cols]
            slant = jnp.broadcast_to(1.0 / (1.66 * mu), (8, LANES))
            square = q_ref[:, cols]
            square = square * square
            for level in range(LEV):
                q_wide[level] = jnp.broadcast_to(square[level:level + 1], (8, LANES))

            def down(level, direct):
                flux[level] = direct
                depth = absb[level] * q_wide[level][None] + rayb[...]
                return direct * jnp.exp2(depth * slant[None])

            direct = lax.fori_loop(0, LEV, down, solb[...], unroll=4)
            partial[LEV] = jnp.sum(direct * (1.0 - alb)[None], axis=0)

            def up(step, below):
                level = LEV - 1 - step
                ray = rayb[...]
                depth = absb[level] * q_wide[level][None] + ray
                diffuse = jnp.exp2(depth)
                half = ray * 0.5
                rho = half - half * diffuse
                rest = depth - rho * below
                through = diffuse * depth
                above = (rho * rest + through * through * below) / (depth * rest)
                partial[level] = jnp.sum(flux[level] * (1.0 - above), axis=0)
                return above

            lax.fori_loop(0, LEV, up, jnp.broadcast_to(alb[None], (G_BLOCKS, 8, LANES)), unroll=4)
            net = jnp.sum(partial[...], axis=1)
            heat = (net[:LEV] - net[1:LEV + 1]) * (72.0 * mu)
            out_ref[:, cols] = jnp.where(lit == 1, heat, 0.0)

        return carry

    lax.fori_loop(0, E // LANES, one_block, 0)
    keep.wait()


def shards(moisture, jacobian, partners, daylit, cos_zenith, albedo, absorb, rayleigh, solar):
    f32 = jnp.float32
    flat = moisture.reshape(LEV * 16, E)
    jac = jacobian.reshape(1, E)
    vmem, anywhere = pl.BlockSpec(memory_space=pltpu.VMEM), pl.BlockSpec(memory_space=pl.ANY)
    tile = (8, LANES)
    new, column_q = pl.pallas_call(
        exchange,
        in_specs=[anywhere] * 3,
        out_specs=[anywhere, vmem],
        out_shape=[jax.ShapeDtypeStruct((LEV * 16, E), f32), jax.ShapeDtypeStruct((LEV, E), f32)],
        scratch_shapes=[
            pltpu.VMEM((GROUPS, 128, E), f32),
            pltpu.VMEM((GROUPS, 8, 128, LANES), f32),
            pltpu.VMEM((GROUPS, 4, 8) + tile, f32),
            pltpu.VMEM((GROUPS, 4, 18) + tile, f32),
            pltpu.VMEM((16,) + tile, f32),
            pltpu.VMEM((5, 8) + tile, f32),
            pltpu.VMEM((2, 8) + tile, jnp.int32),
            pltpu.VMEM((2, 8) + tile, jnp.int32),
            pltpu.VMEM((1, E), f32),
            pltpu.VMEM((2, E), jnp.int32),
            pltpu.SemaphoreType.DMA((GROUPS + 2,)),
            pltpu.SemaphoreType.DMA((GROUPS,)),
            pltpu.SemaphoreType.DMA((2, GROUPS + 1)),
            pltpu.SemaphoreType.DMA((2, GROUPS + 1)),
        ],
        compiler_params=pltpu.CompilerParams(collective_id=0, has_side_effects=True, vmem_limit_bytes=60 * 2**20),
        name="exchange",
    )(flat, jac, partners)
    heating, new = pl.pallas_call(
        radiate,
        in_specs=[anywhere] + [vmem] * 6 + [anywhere],
        out_specs=[vmem, anywhere],
        out_shape=[jax.ShapeDtypeStruct((LEV, E), f32), jax.ShapeDtypeStruct((LEV * 16, E), f32)],
        scratch_shapes=[
            pltpu.VMEM((LEV, G_BLOCKS, 8, LANES), f32),
            pltpu.VMEM((G_BLOCKS, 8, LANES), f32),
            pltpu.VMEM((G_BLOCKS, 8, LANES), f32),
            pltpu.VMEM((LEV, G_BLOCKS, 8, LANES), f32),
            pltpu.VMEM((LEV + 1, 8, LANES), f32),
            pltpu.VMEM((LEV, 8, LANES), f32),
            pltpu.VMEM((LEV, E), f32),
            pltpu.SemaphoreType.DMA,
            pltpu.SemaphoreType.DMA,
        ],
        compiler_params=pltpu.CompilerParams(vmem_limit_bytes=60 * 2**20),
        name="radiate",
    )(
        column_q,
        cos_zenith.reshape(1, E),
        albedo.reshape(1, E),
        daylit.reshape(1, E),
        absorb.T,
        rayleigh.reshape(1, G),
        solar.reshape(1, G),
        new,
    )
    return (new.reshape(LEV, 16, E), heating)


def solution(mesh):
    columns = P(("group", "curve"))
    placed = (
        P(None, None, ("group", "curve")),
        columns,
        P(None, ("group", "curve")),
        columns,
        columns,
        columns,
        P(),
        P(),
        P(),
    )
    return jax.shard_map(
        shards,
        mesh=mesh,
        in_specs=placed,
        out_specs=(P(None, None, ("group", "curve")), P(None, ("group", "curve"))),
        check_vma=False,
    )
```

time: 71.5 us -> 164 us (2.29)
  Pallas kernels: 54.4 us -> 163 us
  waiting for transfers between devices: 7.8 us -> 0 us
  starting transfers between devices: 5.13 us -> 0 us
  local copies, waits for them, and re-layouts: 2.96 us -> 0 us
    pallas_call x3 -> x2, Pallas kernels: 54.4 us -> 163 us  [the longest x1 146 us: shards(): pl.pallas_call(radiate, in_specs=[anywhere] + [vmem] * 6 + [anywhere], ou...]
    ppermute x2 -> x0, waiting for transfers between devices: 7.8 us -> none  [the longest x1 7.8 us: shards(): lax.ppermute(tail, 'curve', [(i, (i + 1) % count) for i in range(count)])]
    ppermute x2 -> x0, starting transfers between devices: 5.13 us -> none  [the longest x1 5.05 us: shards(): lax.ppermute(head, 'curve', [((i + 1) % count, i) for i in range(count)])]
    unnamed x19 -> x0, local copies, waits for them, and re-layouts: 2.75 us -> none
  transfers between devices with their start and end apart: 2 -> 0, of which waited for: 1 -> 0; matrix products, arithmetic and copies ran while one was open for 0% -> 0% of each run, Pallas kernels for 0% -> 0%
where the time goes in v2:
time: 164 us; the launch traced here: 163 us
  Pallas kernels  163 us (99%)
    pallas_call x1, Pallas kernels, shards(): pl.pallas_call(radiate, in_specs=[anywhere] + [vmem] * 6 + [anywhere], ou...  146 us
    pallas_call x1, Pallas kernels, shards(): pl.pallas_call(exchange, in_specs=[anywhere] * 3, out_specs=[anywhere, vm...  17.2 us

profile of v2, /device:TPU:0, one launch (start us, length us, event | category | flops | bytes accessed | tf_op | source)
XLA Modules:
  0.0 163.4 jit_solution(4475781846162816875)
XLA Ops:
  0.6 17.2 %exchange.1 = (f32[1152,1024]{1,0:T(8,128)}, f32[72,1024]{1,0:T(8,128)}) custom-call(f32[1152,1024]{1,0:T(8,128)} %bitcast.9, f32[1,1024]{1,0:T(1,128)} %bitcast.11, s32[2,1024]{1,0:T(2,128)} %partner_hbm.1), custom_call_target="tpu_custom_call" | custom-call | tf_op jit(solution)/shard_map/exchange/pallas_call | solution.py:262
  17.8 145.6 %radiate.1 = (f32[72,1024]{1,0:T(8,128)}, f32[1152,1024]{1,0:T(8,128)}) custom-call(f32[72,1024]{1,0:T(8,128)} %get-tuple-element.6.q_hbm, f32[1,1024]{1,0:T(1,128)} %bitcast.12, f32[1,1024]{1,0:T(1,128)} %bitcast.13, s32[1,1024]{1,0:T(1,128)} %bitcast.14, f32[72,112]{1,0:T(8,128)} %bitcast.10, f32[1,112]{1,0:T(1,128)} %bitcast.15, f32[1,112]{1,0:T(1,128)} %bitcast.16, ...), custom_call_target="tpu_custom_call" | custom-call | tf_op jit(solution)/shard_map/radiate/pallas_call | solution.py:286

commit v3 on v2

--- a/solution.py
+++ b/solution.py
@@ -13,6 +13,10 @@
 CROSSED = (1, 2, 13, 14)
 SIDES = (4, 8, 7, 11)
 G_BLOCKS = G // 8
+CHAINS = G_BLOCKS // 2
+STEP = 8
+STEPS = LEV // STEP
+RAYS = 4
 EXPONENT = -1.66 * 1.4426950408889634
 
 
@@ -189,67 +193,148 @@
     lax.fori_loop(0, GROUPS, finish, 0)
 
 
-def radiate(q_hbm, mu_ref, alb_ref, lit_ref, absorb_ref, ray_ref, solar_ref, new_ref, out_ref, kept_ref, absb, rayb, solb, flux, partial, q_wide, q_ref, kept_sem, q_sem):
+def summands(x, count):
+    parts = []
+    for _ in range(count):
+        parts.append(x.astype(jnp.bfloat16).astype(jnp.float32))
+        x = x - parts[-1]
+    return parts
+
+
+def short_summands(x, count):
+    parts = []
+    for _ in range(count):
+        big = x * float(2**20 + 1)
+        parts.append(big - (big - x))
+        x = x - parts[-1]
+    return parts
+
+
+def build_left(left, absorb, ray, solar):
+    high, low = summands(absorb, 2)
+    rays = short_summands(ray, RAYS)
+    logs = summands(jnp.log2(solar), 3)
+    used = 3 * LEV + 2 * RAYS + 6
+    source = jnp.concatenate(
+        [high, high, low] + rays + rays + [logs[0], logs[0], logs[1], logs[1], logs[2], logs[0]]
+        + [jnp.zeros((G, 256 - used), jnp.float32)],
+        axis=1,
+    ).astype(jnp.bfloat16)
+    column = lax.broadcasted_iota(jnp.int32, (1, 256), 1)
+    level_of = jnp.where(column < LEV, column, jnp.where(column < 2 * LEV, column - LEV, column - 2 * LEV))
+    absorbs = column < 3 * LEV
+    eights = (column >= 3 * LEV) & (column < 3 * LEV + RAYS)
+    ones = (column >= 3 * LEV + RAYS) & (column < 3 * LEV + 2 * RAYS)
+    for level in range(LEV):
+        step, i = divmod(LEV - 1 - level, STEP)
+        single = jnp.where(absorbs, (level_of == level).astype(jnp.float32), jnp.where(ones, 1.0, 0.0))
+        tens, units = divmod(level + 1, 8)
+        rest = jnp.where(eights, float(tens), jnp.where(ones, float(units), 1.0))
+        summed = jnp.where(absorbs, (level_of <= level).astype(jnp.float32), rest)
+        for kind, mask in enumerate((single, summed)):
+            rows = pl.ds((kind * STEP + i) * G, G)
+            left[step, rows, :] = source * jnp.broadcast_to(mask, (G, 256)).astype(jnp.bfloat16)
+
+
+def build_right(q, mu):
+    high, low = summands(q * q, 2)
+    cos = summands(1.66 * mu, 3)
+    one = jnp.ones((RAYS, LANES), jnp.float32)
+    used = 3 * LEV + 2 * RAYS + 6
+    rows = [high, low, high, one * 8.0, one, cos[0], cos[1], cos[0], cos[1], cos[0], cos[2]]
+    return jnp.concatenate(rows + [jnp.zeros((256 - used, LANES), jnp.float32)], axis=0).astype(jnp.bfloat16)
+
+
+def radiate(
+    q_hbm, mu_ref, alb_ref, lit_ref, absorb_ref, ray_ref, solar_ref, new_hbm, out_ref, kept_hbm,
+    left, right, half_ray, top, even, odd, climbing, net, q_ref, new_ref, q_sem, new_sem, kept_sem,
+):
     fetch = pltpu.make_async_copy(q_hbm, q_ref, q_sem)
+    land = pltpu.make_async_copy(new_hbm, new_ref, new_sem)
+    keep = pltpu.make_async_copy(new_ref, kept_hbm, kept_sem)
     fetch.start()
-    keep = pltpu.make_async_copy(new_ref, kept_ref, kept_sem)
+    land.start()
+    lit_count = jnp.sum(lit_ref[...])
+    pairs = E // (2 * LANES)
+
+    @pl.when(lit_count > 0)
+    def _():
+        ray = ray_ref[...].T * EXPONENT
+        solar = solar_ref[...].T
+        build_left(left, absorb_ref[...].T * EXPONENT, ray, solar)
+        half_ray[...] = jnp.broadcast_to(ray * 0.5, (G, LANES)).reshape(G_BLOCKS, 8, LANES)
+        top[...] = jnp.broadcast_to(solar, (G, LANES)).reshape(G_BLOCKS, 8, LANES)
+
+    fetch.wait()
+    land.wait()
     keep.start()
-    scaled = absorb_ref[...].T * EXPONENT
-    for level in range(LEV):
-        absb[level] = jnp.broadcast_to(scaled[:, level:level + 1], (G, LANES)).reshape(G_BLOCKS, 8, LANES)
-    rayb[...] = jnp.broadcast_to(ray_ref[...].T * EXPONENT, (G, LANES)).reshape(G_BLOCKS, 8, LANES)
-    solb[...] = jnp.broadcast_to(solar_ref[...].T, (G, LANES)).reshape(G_BLOCKS, 8, LANES)
-
-    fetch.wait()
-
-    def one_block(block, carry):
-        cols = pl.ds(pl.multiple_of(block * LANES, LANES), LANES)
-        lit = lit_ref[0:1, cols]
-        count = jnp.sum(lit)
-
-        @pl.when(count == 0)
+
+    def columns(pair, b):
+        return pl.ds(pl.multiple_of((2 * pair + b) * LANES, LANES), LANES)
+
+    def depths(n, buffer):
+        pair, step = lax.div(n, STEPS), lax.rem(n, STEPS)
+        buffer[...] = jnp.dot(left[step], right[pair], preferred_element_type=jnp.float32)
+
+    def climb(n, buffer, following, next_buffer):
+        pair, step = lax.div(n, STEPS), lax.rem(n, STEPS)
+
+        @pl.when(step == 0)
         def _():
-            out_ref[:, cols] = jnp.zeros((LEV, LANES), jnp.float32)
-
-        @pl.when(count > 0)
+            for b in range(2):
+                climbing[b] = jnp.broadcast_to(alb_ref[0:1, columns(pair, b)][None], (G_BLOCKS, 8, LANES))
+
+        totals = {}
+        for b in range(2):
+            lanes = slice(b * LANES, (b + 1) * LANES)
+            slant = jnp.broadcast_to(1.0 / (1.66 * mu_ref[0:1, columns(pair, b)]), (8, LANES))[None]
+            for half in range(2):
+                chains = pl.ds(half * CHAINS, CHAINS)
+                below = climbing[b, chains]
+                ray = half_ray[chains]
+                for i in range(STEP):
+                    level = LEV - 1 - step * STEP - i
+                    first = i * G + half * CHAINS * 8
+                    second_kind = first + STEP * G
+                    depth = buffer[first:first + CHAINS * 8, lanes].reshape(CHAINS, 8, LANES)
+                    above_it = buffer[second_kind:second_kind + CHAINS * 8, lanes].reshape(CHAINS, 8, LANES)
+                    totals[half, i] = jnp.sum(jnp.exp2(above_it * slant) * (1.0 - below), axis=0)
+                    if half == 1:
+                        net[b, level + 1] = totals[0, i] + totals[1, i]
+                    diffuse = jnp.exp2(depth)
+                    reflect = (ray - ray * diffuse) * (1.0 / depth)
+                    below = reflect + diffuse * diffuse * below * (1.0 / (1.0 - reflect * below))
+                climbing[b, chains] = below
+        depths(following, next_buffer)
+
+        @pl.when(step == STEPS - 1)
         def _():
-            mu = mu_ref[0:1, cols]
-            alb = alb_ref[0:1, cols]
-            slant = jnp.broadcast_to(1.0 / (1.66 * mu), (8, LANES))
-            square = q_ref[:, cols]
-            square = square * square
-            for level in range(LEV):
-                q_wide[level] = jnp.broadcast_to(square[level:level + 1], (8, LANES))
-
-            def down(level, direct):
-                flux[level] = direct
-                depth = absb[level] * q_wide[level][None] + rayb[...]
-                return direct * jnp.exp2(depth * slant[None])
-
-            direct = lax.fori_loop(0, LEV, down, solb[...], unroll=4)
-            partial[LEV] = jnp.sum(direct * (1.0 - alb)[None], axis=0)
-
-            def up(step, below):
-                level = LEV - 1 - step
-                ray = rayb[...]
-                depth = absb[level] * q_wide[level][None] + ray
-                diffuse = jnp.exp2(depth)
-                half = ray * 0.5
-                rho = half - half * diffuse
-                rest = depth - rho * below
-                through = diffuse * depth
-                above = (rho * rest + through * through * below) / (depth * rest)
-                partial[level] = jnp.sum(flux[level] * (1.0 - above), axis=0)
-                return above
-
-            lax.fori_loop(0, LEV, up, jnp.broadcast_to(alb[None], (G_BLOCKS, 8, LANES)), unroll=4)
-            net = jnp.sum(partial[...], axis=1)
-            heat = (net[:LEV] - net[1:LEV + 1]) * (72.0 * mu)
-            out_ref[:, cols] = jnp.where(lit == 1, heat, 0.0)
-
-        return carry
-
-    lax.fori_loop(0, E // LANES, one_block, 0)
+            for b in range(2):
+                cols = columns(pair, b)
+                net[b, 0] = jnp.sum(top[...] * (1.0 - climbing[b]), axis=0)
+                total = jnp.sum(net[b], axis=1)
+                heat = (total[:LEV] - total[1:]) * (72.0 * mu_ref[0:1, cols])
+                out_ref[:, cols] = jnp.where(lit_ref[0:1, cols] == 1, heat, 0.0)
+
+    @pl.when(lit_count > 0)
+    def _():
+        for pair in range(pairs):
+            for b in range(2):
+                cols = slice((2 * pair + b) * LANES, (2 * pair + b + 1) * LANES)
+                right[pair, :, b * LANES:(b + 1) * LANES] = build_right(q_ref[:, cols], mu_ref[0:1, cols])
+        depths(jnp.int32(0), even)
+
+        def two_steps(k, carry):
+            climb(2 * k, even, 2 * k + 1, odd)
+            climb(2 * k + 1, odd, jnp.minimum(2 * k + 2, pairs * STEPS - 1), even)
+            return carry
+
+        lax.fori_loop(0, pairs * STEPS // 2, two_steps, 0)
+
+    @pl.when(lit_count == 0)
+    def _():
+        out_ref[...] = jnp.zeros((LEV, E), jnp.float32)
+
     keep.wait()
 
 
@@ -289,13 +374,17 @@
         out_specs=[vmem, anywhere],
         out_shape=[jax.ShapeDtypeStruct((LEV, E), f32), jax.ShapeDtypeStruct((LEV * 16, E), f32)],
         scratch_shapes=[
-            pltpu.VMEM((LEV, G_BLOCKS, 8, LANES), f32),
-            pltpu.VMEM((G_BLOCKS, 8, LANES), f32),
-            pltpu.VMEM((G_BLOCKS, 8, LANES), f32),
-            pltpu.VMEM((LEV, G_BLOCKS, 8, LANES), f32),
-            pltpu.VMEM((LEV + 1, 8, LANES), f32),
-            pltpu.VMEM((LEV, 8, LANES), f32),
+            pltpu.VMEM((STEPS, 2 * STEP * G, 256), jnp.bfloat16),
+            pltpu.VMEM((E // 256, 256, 256), jnp.bfloat16),
+            pltpu.VMEM((G_BLOCKS,) + tile, f32),
+            pltpu.VMEM((G_BLOCKS,) + tile, f32),
+            pltpu.VMEM((2 * STEP * G, 256), f32),
+            pltpu.VMEM((2 * STEP * G, 256), f32),
+            pltpu.VMEM((2, G_BLOCKS) + tile, f32),
+            pltpu.VMEM((2, LEV + 1) + tile, f32),
             pltpu.VMEM((LEV, E), f32),
+            pltpu.VMEM((LEV * 16, E), f32),
+            pltpu.SemaphoreType.DMA,
             pltpu.SemaphoreType.DMA,
             pltpu.SemaphoreType.DMA,
         ],

time: 164 us -> 46.3 us (0.28)
  Pallas kernels: 163 us -> 45.5 us
    pallas_call x1, Pallas kernels: 146 us -> 28.3 us  [shards(): pl.pallas_call(radiate, in_specs=[anywhere] + [vmem] * 6 + [anywhere], ou...]
where the time goes in v3:
time: 46.3 us; the launch traced here: 46.1 us
  Pallas kernels  45.5 us (98%)
  between operations  0.64 us (1%)
    pallas_call x1, Pallas kernels, shards(): pl.pallas_call(radiate, in_specs=[anywhere] + [vmem] * 6 + [anywhere], ou...  28.3 us
    pallas_call x1, Pallas kernels, shards(): pl.pallas_call(exchange, in_specs=[anywhere] * 3, out_specs=[anywhere, vm...  17.2 us

profile of v3, /device:TPU:0, one launch (start us, length us, event | category | flops | bytes accessed | tf_op | source)
XLA Modules:
  0.0 46.1 jit_solution(11814312924092140651)
XLA Ops:
  0.6 17.2 %exchange.1 = (f32[1152,1024]{1,0:T(8,128)}, f32[72,1024]{1,0:T(8,128)}) custom-call(f32[1152,1024]{1,0:T(8,128)} %bitcast.9, f32[1,1024]{1,0:T(1,128)} %bitcast.11, s32[2,1024]{1,0:T(2,128)} %partner_hbm.1), custom_call_target="tpu_custom_call" | custom-call | tf_op jit(solution)/shard_map/exchange/pallas_call | solution.py:347
  17.8 28.3 %radiate.1 = (f32[72,1024]{1,0:T(8,128)}, f32[1152,1024]{1,0:T(8,128)}) custom-call(f32[72,1024]{1,0:T(8,128)} %get-tuple-element.6.q_hbm, f32[1,1024]{1,0:T(1,128)} %bitcast.12, f32[1,1024]{1,0:T(1,128)} %bitcast.13, s32[1,1024]{1,0:T(1,128)} %bitcast.14, f32[72,112]{1,0:T(8,128)} %bitcast.10, f32[1,112]{1,0:T(1,128)} %bitcast.15, f32[1,112]{1,0:T(1,128)} %bitcast.16, ...), custom_call_target="tpu_custom_call" | custom-call | tf_op jit(solution)/shard_map/radiate/pallas_call | solution.py:371

commit v4 on v3

--- a/solution.py
+++ b/solution.py
@@ -17,6 +17,7 @@
 STEP = 8
 STEPS = LEV // STEP
 RAYS = 4
+AHEAD = 3
 EXPONENT = -1.66 * 1.4426950408889634
 
 
@@ -78,7 +79,7 @@
     ]
     for copy in small:
         copy.start()
-    for group in range(GROUPS):
+    for group in range(AHEAD):
         fetch(group).start()
     for copy in small:
         copy.wait()
@@ -91,11 +92,8 @@
             index = (jnp.broadcast_to(partner_ref[side:side + 1, cols], (8, LANES)) + HALF) & (E - 1)
             inside[side, block] = index & (LANES - 1)
             slot[side, block] = index >> 7
-    pl.semaphore_wait(barrier, 2)
-    for way in range(2):
-        send_jacobian(way).start()
-
-    def first_part(group, carry):
+
+    def first_part(group):
         fetch(group).wait()
         for block in range(blocks):
             cols = pl.ds(block * LANES, LANES)
@@ -127,11 +125,26 @@
                 else:
                     inner = inner + new
             q_ref[pl.ds(pl.multiple_of(group * 8, 8), 8), cols] = corner * (1.0 / 144.0) + inner * (25.0 / 144.0)
+
+    first_part(0)
+    pl.semaphore_wait(barrier, 2)
+    for way in range(2):
+        send_jacobian(way).start()
+        send(way, 0).start()
+    for group in range(AHEAD, AHEAD + 1):
+        fetch(group).start()
+
+    def next_group(group, carry):
+        @pl.when(group + AHEAD < GROUPS)
+        def _():
+            fetch(group + AHEAD).start()
+
+        first_part(group)
         for way in range(2):
             send(way, group).start()
         return carry
 
-    lax.fori_loop(0, GROUPS, first_part, 0)
+    lax.fori_loop(1, GROUPS, next_group, 0)
 
     def gather(side, block, window):
         where, which = inside[side, block], slot[side, block]
@@ -266,15 +279,15 @@
         top[...] = jnp.broadcast_to(solar, (G, LANES)).reshape(G_BLOCKS, 8, LANES)
 
     fetch.wait()
-    land.wait()
-    keep.start()
 
     def columns(pair, b):
         return pl.ds(pl.multiple_of((2 * pair + b) * LANES, LANES), LANES)
 
-    def depths(n, buffer):
+    def depths(n, buffer, piece, pieces):
         pair, step = lax.div(n, STEPS), lax.rem(n, STEPS)
-        buffer[...] = jnp.dot(left[step], right[pair], preferred_element_type=jnp.float32)
+        size = 2 * STEP * G // pieces
+        rows = slice(piece * size, (piece + 1) * size)
+        buffer[rows, :] = jnp.dot(left[step, rows, :], right[pair], preferred_element_type=jnp.float32)
 
     def climb(n, buffer, following, next_buffer):
         pair, step = lax.div(n, STEPS), lax.rem(n, STEPS)
@@ -284,28 +297,29 @@
             for b in range(2):
                 climbing[b] = jnp.broadcast_to(alb_ref[0:1, columns(pair, b)][None], (G_BLOCKS, 8, LANES))
 
-        totals = {}
+        below, totals = {}, {}
         for b in range(2):
             lanes = slice(b * LANES, (b + 1) * LANES)
             slant = jnp.broadcast_to(1.0 / (1.66 * mu_ref[0:1, columns(pair, b)]), (8, LANES))[None]
             for half in range(2):
-                chains = pl.ds(half * CHAINS, CHAINS)
-                below = climbing[b, chains]
-                ray = half_ray[chains]
-                for i in range(STEP):
-                    level = LEV - 1 - step * STEP - i
+                below[half] = climbing[b, pl.ds(half * CHAINS, CHAINS)]
+            for i in range(STEP):
+                if i % (STEP // 2) == 0:
+                    depths(following, next_buffer, 2 * b + i // (STEP // 2), 4)
+                level = LEV - 1 - step * STEP - i
+                for half in range(2):
+                    ray = half_ray[pl.ds(half * CHAINS, CHAINS)]
                     first = i * G + half * CHAINS * 8
                     second_kind = first + STEP * G
                     depth = buffer[first:first + CHAINS * 8, lanes].reshape(CHAINS, 8, LANES)
                     above_it = buffer[second_kind:second_kind + CHAINS * 8, lanes].reshape(CHAINS, 8, LANES)
-                    totals[half, i] = jnp.sum(jnp.exp2(above_it * slant) * (1.0 - below), axis=0)
-                    if half == 1:
-                        net[b, level + 1] = totals[0, i] + totals[1, i]
+                    totals[half] = jnp.sum(jnp.exp2(above_it * slant) * (1.0 - below[half]), axis=0)
                     diffuse = jnp.exp2(depth)
                     reflect = (ray - ray * diffuse) * (1.0 / depth)
-                    below = reflect + diffuse * diffuse * below * (1.0 / (1.0 - reflect * below))
-                climbing[b, chains] = below
-        depths(following, next_buffer)
+                    below[half] = reflect + diffuse * diffuse * below[half] * (1.0 / (1.0 - reflect * below[half]))
+                net[b, level + 1] = totals[0] + totals[1]
+            for half in range(2):
+                climbing[b, pl.ds(half * CHAINS, CHAINS)] = below[half]
 
         @pl.when(step == STEPS - 1)
         def _():
@@ -322,9 +336,14 @@
             for b in range(2):
                 cols = slice((2 * pair + b) * LANES, (2 * pair + b + 1) * LANES)
                 right[pair, :, b * LANES:(b + 1) * LANES] = build_right(q_ref[:, cols], mu_ref[0:1, cols])
-        depths(jnp.int32(0), even)
+        depths(jnp.int32(0), even, 0, 1)
 
         def two_steps(k, carry):
+            @pl.when(k == 2)
+            def _():
+                land.wait()
+                keep.start()
+
             climb(2 * k, even, 2 * k + 1, odd)
             climb(2 * k + 1, odd, jnp.minimum(2 * k + 2, pairs * STEPS - 1), even)
             return carry
@@ -333,6 +352,8 @@
 
     @pl.when(lit_count == 0)
     def _():
+        land.wait()
+        keep.start()
         out_ref[...] = jnp.zeros((LEV, E), jnp.float32)
 
     keep.wait()

time: 46.3 us -> 43.4 us (0.937)
  Pallas kernels: 45.5 us -> 42.5 us
    pallas_call x1, Pallas kernels: 28.3 us -> 25.1 us  [shards(): pl.pallas_call(radiate, in_specs=[anywhere] + [vmem] * 6 + [anywhere], ou...]
where the time goes in v4:
time: 43.4 us; the launch traced here: 43.1 us
  Pallas kernels  42.5 us (98%)
  between operations  0.64 us (1%)
    pallas_call x1, Pallas kernels, shards(): pl.pallas_call(radiate, in_specs=[anywhere] + [vmem] * 6 + [anywhere], ou...  25.1 us
    pallas_call x1, Pallas kernels, shards(): pl.pallas_call(exchange, in_specs=[anywhere] * 3, out_specs=[anywhere, vm...  17.3 us

profile of v4, /device:TPU:0, one launch (start us, length us, event | category | flops | bytes accessed | tf_op | source)
XLA Modules:
  0.0 43.1 jit_solution(17963502643230860464)
XLA Ops:
  0.6 17.3 %exchange.1 = (f32[1152,1024]{1,0:T(8,128)}, f32[72,1024]{1,0:T(8,128)}) custom-call(f32[1152,1024]{1,0:T(8,128)} %bitcast.9, f32[1,1024]{1,0:T(1,128)} %bitcast.11, s32[2,1024]{1,0:T(2,128)} %partner_hbm.1), custom_call_target="tpu_custom_call" | custom-call | tf_op jit(solution)/shard_map/exchange/pallas_call | solution.py:368
  18.0 25.1 %radiate.1 = (f32[72,1024]{1,0:T(8,128)}, f32[1152,1024]{1,0:T(8,128)}) custom-call(f32[72,1024]{1,0:T(8,128)} %get-tuple-element.6.q_hbm, f32[1,1024]{1,0:T(1,128)} %bitcast.12, f32[1,1024]{1,0:T(1,128)} %bitcast.13, s32[1,1024]{1,0:T(1,128)} %bitcast.14, f32[72,112]{1,0:T(8,128)} %bitcast.10, f32[1,112]{1,0:T(1,128)} %bitcast.15, f32[1,112]{1,0:T(1,128)} %bitcast.16, ...), custom_call_target="tpu_custom_call" | custom-call | tf_op jit(solution)/shard_map/radiate/pallas_call | solution.py:392

commit v5 on v4

--- a/solution.py
+++ b/solution.py
@@ -16,7 +16,9 @@
 CHAINS = G_BLOCKS // 2
 STEP = 8
 STEPS = LEV // STEP
-RAYS = 4
+EIGHTS = 3 * LEV
+ONES = EIGHTS + 6
+LOGS = ONES + 6
 AHEAD = 3
 EXPONENT = -1.66 * 1.4426950408889634
 
@@ -113,10 +115,6 @@
                 if n in SIDES:
                     k = SIDES.index(n)
                     sides[group, k, block] = value
-                    if block == 0 and k < 2:
-                        crossed[group, 1, 16 + k] = value
-                    if block == blocks - 1 and k >= 2:
-                        crossed[group, 2, 16 + k - 2] = value
                     continue
                 new = node[n] + inverse * value
                 made[group, block, pl.ds(n, 8, stride=16), :] = new
@@ -125,6 +123,10 @@
                 else:
                     inner = inner + new
             q_ref[pl.ds(pl.multiple_of(group * 8, 8), 8), cols] = corner * (1.0 / 144.0) + inner * (25.0 / 144.0)
+        crossed[group, 1, 16] = jnp.where(lane == 0, sides[group, 0, 0], pltpu.roll(sides[group, 1, 0], 1, 1))
+        crossed[group, 2, 16] = jnp.where(
+            lane == LANES - 1, sides[group, 2, blocks - 1], pltpu.roll(sides[group, 3, blocks - 1], LANES - 1, 1)
+        )
 
     first_part(0)
     pl.semaphore_wait(barrier, 2)
@@ -175,13 +177,17 @@
             section, place = 1 + block // 4, (block % 4) * 4
             others = []
             for a in range(2):
-                last = crossed[group, 0, 16 + a] if block == 0 else sides[group, 2 + a, block - 1]
-                others.append(jnp.where(lane == 0, pltpu.roll(last, 1, 1), pltpu.roll(sides[group, 2 + a, block], 1, 1)))
+                if block == 0:
+                    carried = pltpu.roll(crossed[group, 0, 16], 1 + a, 1)
+                else:
+                    carried = pltpu.roll(sides[group, 2 + a, block - 1], 1, 1)
+                others.append(jnp.where(lane == 0, carried, pltpu.roll(sides[group, 2 + a, block], 1, 1)))
             for a in range(2):
-                following = crossed[group, 3, 16 + a] if block == blocks - 1 else sides[group, a, block + 1]
-                others.append(
-                    jnp.where(lane == LANES - 1, pltpu.roll(following, LANES - 1, 1), pltpu.roll(sides[group, a, block], LANES - 1, 1))
-                )
+                if block == blocks - 1:
+                    carried = pltpu.roll(crossed[group, 3, 16], LANES - 1 - a, 1)
+                else:
+                    carried = pltpu.roll(sides[group, a, block + 1], LANES - 1, 1)
+                others.append(jnp.where(lane == LANES - 1, carried, pltpu.roll(sides[group, a, block], LANES - 1, 1)))
             for side in range(2):
                 def window(k):
                     return [crossed[group, 2 * (block // 4) + k // 4, (k % 4) * 4 + 2 * side + c] for c in (1, 0)]
@@ -225,37 +231,40 @@
 
 def build_left(left, absorb, ray, solar):
     high, low = summands(absorb, 2)
-    rays = short_summands(ray, RAYS)
-    logs = summands(jnp.log2(solar), 3)
-    used = 3 * LEV + 2 * RAYS + 6
+    rays = short_summands(ray, 4)
+    rays = rays + rays[:2]
     source = jnp.concatenate(
-        [high, high, low] + rays + rays + [logs[0], logs[0], logs[1], logs[1], logs[2], logs[0]]
-        + [jnp.zeros((G, 256 - used), jnp.float32)],
-        axis=1,
+        [high, high, low] + rays + rays + summands(jnp.log2(solar), 3) + [jnp.zeros((G, 256 - LOGS - 3), jnp.float32)], axis=1
     ).astype(jnp.bfloat16)
     column = lax.broadcasted_iota(jnp.int32, (1, 256), 1)
     level_of = jnp.where(column < LEV, column, jnp.where(column < 2 * LEV, column - LEV, column - 2 * LEV))
-    absorbs = column < 3 * LEV
-    eights = (column >= 3 * LEV) & (column < 3 * LEV + RAYS)
-    ones = (column >= 3 * LEV + RAYS) & (column < 3 * LEV + 2 * RAYS)
-    for level in range(LEV):
-        step, i = divmod(LEV - 1 - level, STEP)
-        single = jnp.where(absorbs, (level_of == level).astype(jnp.float32), jnp.where(ones, 1.0, 0.0))
-        tens, units = divmod(level + 1, 8)
-        rest = jnp.where(eights, float(tens), jnp.where(ones, float(units), 1.0))
-        summed = jnp.where(absorbs, (level_of <= level).astype(jnp.float32), rest)
-        for kind, mask in enumerate((single, summed)):
-            rows = pl.ds((kind * STEP + i) * G, G)
-            left[step, rows, :] = source * jnp.broadcast_to(mask, (G, 256)).astype(jnp.bfloat16)
-
-
-def build_right(q, mu):
-    high, low = summands(q * q, 2)
-    cos = summands(1.66 * mu, 3)
-    one = jnp.ones((RAYS, LANES), jnp.float32)
-    used = 3 * LEV + 2 * RAYS + 6
-    rows = [high, low, high, one * 8.0, one, cos[0], cos[1], cos[0], cos[1], cos[0], cos[2]]
-    return jnp.concatenate(rows + [jnp.zeros((256 - used, LANES), jnp.float32)], axis=0).astype(jnp.bfloat16)
+    absorbs = column < EIGHTS
+    eights = column < ONES
+    ones = column < LOGS
+
+    def one_step(step, carry):
+        for i in range(STEP):
+            level = LEV - 1 - step * STEP - i
+            single = jnp.where(absorbs, jnp.where(level_of == level, 1.0, 0.0), jnp.where(eights, 0.0, jnp.where(ones, 1.0, 0.0)))
+            tens = (STEPS - step - (1 if i else 0)).astype(jnp.float32)
+            units = float(STEP - i if i else 0)
+            rest = jnp.where(eights, tens, jnp.where(ones, units, 1.0))
+            summed = jnp.where(absorbs, jnp.where(level_of <= level, 1.0, 0.0), rest)
+            for kind, mask in enumerate((single, summed)):
+                rows = pl.ds((kind * STEP + i) * G, G)
+                left[step, rows, :] = source * jnp.broadcast_to(mask, (G, 256)).astype(jnp.bfloat16)
+        return carry
+
+    lax.fori_loop(0, STEPS, one_step, 0)
+
+
+def build_right(square, ray_weights, log_weight):
+    high, low = summands(square, 2)
+    one = jnp.ones((1, LANES), jnp.float32)
+    first, second_part = (one * part for part in ray_weights)
+    weights = jnp.concatenate([first] * 4 + [second_part] * 2, axis=0)
+    rows = [high, low, high, weights * 8.0, weights, jnp.broadcast_to(one * log_weight, (256 - LOGS, LANES))]
+    return jnp.concatenate(rows, axis=0).astype(jnp.bfloat16)
 
 
 def radiate(
@@ -283,11 +292,11 @@
     def columns(pair, b):
         return pl.ds(pl.multiple_of((2 * pair + b) * LANES, LANES), LANES)
 
-    def depths(n, buffer, piece, pieces):
+    def depths(n, buffer, piece):
         pair, step = lax.div(n, STEPS), lax.rem(n, STEPS)
-        size = 2 * STEP * G // pieces
+        size = 2 * STEP * G // 4
         rows = slice(piece * size, (piece + 1) * size)
-        buffer[rows, :] = jnp.dot(left[step, rows, :], right[pair], preferred_element_type=jnp.float32)
+        buffer[rows, :] = jnp.dot(left[step, rows, :], right[piece // 2, pair], preferred_element_type=jnp.float32)
 
     def climb(n, buffer, following, next_buffer):
         pair, step = lax.div(n, STEPS), lax.rem(n, STEPS)
@@ -300,12 +309,11 @@
         below, totals = {}, {}
         for b in range(2):
             lanes = slice(b * LANES, (b + 1) * LANES)
-            slant = jnp.broadcast_to(1.0 / (1.66 * mu_ref[0:1, columns(pair, b)]), (8, LANES))[None]
             for half in range(2):
                 below[half] = climbing[b, pl.ds(half * CHAINS, CHAINS)]
             for i in range(STEP):
                 if i % (STEP // 2) == 0:
-                    depths(following, next_buffer, 2 * b + i // (STEP // 2), 4)
+                    depths(following, next_buffer, 2 * b + i // (STEP // 2))
                 level = LEV - 1 - step * STEP - i
                 for half in range(2):
                     ray = half_ray[pl.ds(half * CHAINS, CHAINS)]
@@ -313,7 +321,7 @@
                     second_kind = first + STEP * G
                     depth = buffer[first:first + CHAINS * 8, lanes].reshape(CHAINS, 8, LANES)
                     above_it = buffer[second_kind:second_kind + CHAINS * 8, lanes].reshape(CHAINS, 8, LANES)
-                    totals[half] = jnp.sum(jnp.exp2(above_it * slant) * (1.0 - below[half]), axis=0)
+                    totals[half] = jnp.sum(jnp.exp2(above_it) * (1.0 - below[half]), axis=0)
                     diffuse = jnp.exp2(depth)
                     reflect = (ray - ray * diffuse) * (1.0 / depth)
                     below[half] = reflect + diffuse * diffuse * below[half] * (1.0 / (1.0 - reflect * below[half]))
@@ -335,8 +343,14 @@
         for pair in range(pairs):
             for b in range(2):
                 cols = slice((2 * pair + b) * LANES, (2 * pair + b + 1) * LANES)
-                right[pair, :, b * LANES:(b + 1) * LANES] = build_right(q_ref[:, cols], mu_ref[0:1, cols])
-        depths(jnp.int32(0), even, 0, 1)
+                square = q_ref[:, cols]
+                square = square * square
+                slant = 1.0 / (1.66 * mu_ref[0:1, cols])
+                lanes = slice(b * LANES, (b + 1) * LANES)
+                right[0, pair, :, lanes] = build_right(square, (1.0, 0.0), 0.0)
+                right[1, pair, :, lanes] = build_right(square * slant, summands(slant, 2), 1.0)
+        for piece in range(4):
+            depths(jnp.int32(0), even, piece)
 
         def two_steps(k, carry):
             @pl.when(k == 2)
@@ -374,7 +388,7 @@
             pltpu.VMEM((GROUPS, 128, E), f32),
             pltpu.VMEM((GROUPS, 8, 128, LANES), f32),
             pltpu.VMEM((GROUPS, 4, 8) + tile, f32),
-            pltpu.VMEM((GROUPS, 4, 18) + tile, f32),
+            pltpu.VMEM((GROUPS, 4, 17) + tile, f32),
             pltpu.VMEM((16,) + tile, f32),
             pltpu.VMEM((5, 8) + tile, f32),
             pltpu.VMEM((2, 8) + tile, jnp.int32),
@@ -396,7 +410,7 @@
         out_shape=[jax.ShapeDtypeStruct((LEV, E), f32), jax.ShapeDtypeStruct((LEV * 16, E), f32)],
         scratch_shapes=[
             pltpu.VMEM((STEPS, 2 * STEP * G, 256), jnp.bfloat16),
-            pltpu.VMEM((E // 256, 256, 256), jnp.bfloat16),
+            pltpu.VMEM((2, E // 256, 256, 256), jnp.bfloat16),
             pltpu.VMEM((G_BLOCKS,) + tile, f32),
             pltpu.VMEM((G_BLOCKS,) + tile, f32),
             pltpu.VMEM((2 * STEP * G, 256), f32),

time: 43.4 us -> 42.7 us (0.984)
  the two profiles are of different devices: /device:TPU:0 before, /device:TPU:32 now
where the time goes in v5:
time: 42.7 us; the launch traced here: 42.5 us
  Pallas kernels  41.8 us (98%)
  between operations  0.64 us (1%)
    pallas_call x1, Pallas kernels, shards(): pl.pallas_call(radiate, in_specs=[anywhere] + [vmem] * 6 + [anywhere], ou...  25 us
    pallas_call x1, Pallas kernels, shards(): pl.pallas_call(exchange, in_specs=[anywhere] * 3, out_specs=[anywhere, vm...  16.9 us

profile of v5, /device:TPU:32, one launch (start us, length us, event | category | flops | bytes accessed | tf_op | source)
XLA Modules:
  0.0 42.5 jit_solution(8961421205379808983)
XLA Ops:
  0.6 16.9 %exchange.1 = (f32[1152,1024]{1,0:T(8,128)}, f32[72,1024]{1,0:T(8,128)}) custom-call(f32[1152,1024]{1,0:T(8,128)} %bitcast.9, f32[1,1024]{1,0:T(1,128)} %bitcast.11, s32[2,1024]{1,0:T(2,128)} %partner_hbm.1), custom_call_target="tpu_custom_call" | custom-call | tf_op jit(solution)/shard_map/exchange/pallas_call | solution.py:382
  17.5 25.0 %radiate.1 = (f32[72,1024]{1,0:T(8,128)}, f32[1152,1024]{1,0:T(8,128)}) custom-call(f32[72,1024]{1,0:T(8,128)} %get-tuple-element.6.q_hbm, f32[1,1024]{1,0:T(1,128)} %bitcast.12, f32[1,1024]{1,0:T(1,128)} %bitcast.13, s32[1,1024]{1,0:T(1,128)} %bitcast.14, f32[72,112]{1,0:T(8,128)} %bitcast.10, f32[1,112]{1,0:T(1,128)} %bitcast.15, f32[1,112]{1,0:T(1,128)} %bitcast.16, ...), custom_call_target="tpu_custom_call" | custom-call | tf_op jit(solution)/shard_map/radiate/pallas_call | solution.py:406

commit v6 on v5

--- a/solution.py
+++ b/solution.py
@@ -14,7 +14,7 @@
 SIDES = (4, 8, 7, 11)
 G_BLOCKS = G // 8
 CHAINS = G_BLOCKS // 2
-STEP = 8
+STEP = 18
 STEPS = LEV // STEP
 EIGHTS = 3 * LEV
 ONES = EIGHTS + 6
@@ -172,22 +172,20 @@
     def second_part(group, carry):
         for way in range(2):
             send(way, group).wait()
+        eastern = [[pltpu.roll(crossed[group, 0, 16], 1 + a, 1) for a in range(2)]]
         for block in range(blocks):
             cols = pl.ds(block * LANES, LANES)
             section, place = 1 + block // 4, (block % 4) * 4
-            others = []
-            for a in range(2):
-                if block == 0:
-                    carried = pltpu.roll(crossed[group, 0, 16], 1 + a, 1)
-                else:
-                    carried = pltpu.roll(sides[group, 2 + a, block - 1], 1, 1)
-                others.append(jnp.where(lane == 0, carried, pltpu.roll(sides[group, 2 + a, block], 1, 1)))
-            for a in range(2):
-                if block == blocks - 1:
-                    carried = pltpu.roll(crossed[group, 3, 16], LANES - 1 - a, 1)
-                else:
-                    carried = pltpu.roll(sides[group, a, block + 1], LANES - 1, 1)
-                others.append(jnp.where(lane == LANES - 1, carried, pltpu.roll(sides[group, a, block], LANES - 1, 1)))
+            eastern.append([pltpu.roll(sides[group, 2 + a, block], 1, 1) for a in range(2)])
+            if block == 0:
+                western = [pltpu.roll(sides[group, a, 0], LANES - 1, 1) for a in range(2)]
+            if block == blocks - 1:
+                later = [pltpu.roll(crossed[group, 3, 16], LANES - 1 - a, 1) for a in range(2)]
+            else:
+                later = [pltpu.roll(sides[group, a, block + 1], LANES - 1, 1) for a in range(2)]
+            others = [jnp.where(lane == 0, eastern[block][a], eastern[block + 1][a]) for a in range(2)]
+            others += [jnp.where(lane == LANES - 1, later[a], western[a]) for a in range(2)]
+            western = later
             for side in range(2):
                 def window(k):
                     return [crossed[group, 2 * (block // 4) + k // 4, (k % 4) * 4 + 2 * side + c] for c in (1, 0)]
@@ -246,8 +244,8 @@
         for i in range(STEP):
             level = LEV - 1 - step * STEP - i
             single = jnp.where(absorbs, jnp.where(level_of == level, 1.0, 0.0), jnp.where(eights, 0.0, jnp.where(ones, 1.0, 0.0)))
-            tens = (STEPS - step - (1 if i else 0)).astype(jnp.float32)
-            units = float(STEP - i if i else 0)
+            tens = lax.div(level + 1, 8).astype(jnp.float32)
+            units = lax.rem(level + 1, 8).astype(jnp.float32)
             rest = jnp.where(eights, tens, jnp.where(ones, units, 1.0))
             summed = jnp.where(absorbs, jnp.where(level_of <= level, 1.0, 0.0), rest)
             for kind, mask in enumerate((single, summed)):
@@ -265,6 +263,22 @@
     weights = jnp.concatenate([first] * 4 + [second_part] * 2, axis=0)
     rows = [high, low, high, weights * 8.0, weights, jnp.broadcast_to(one * log_weight, (256 - LOGS, LANES))]
     return jnp.concatenate(rows, axis=0).astype(jnp.bfloat16)
+
+
+def sublane_sums(arrays):
+    row = lax.broadcasted_iota(jnp.int32, (8, LANES), 0)
+    for size in (4, 2, 1):
+        lower = (row & size) == 0
+        joined = []
+        for x, y in zip(arrays[:size], arrays[size:]):
+            swapped = jnp.where(lower, y, x)
+            if size == 4:
+                moved = pltpu.roll(swapped, 4, 0)
+            else:
+                moved = jnp.where(lower, pltpu.roll(swapped, 8 - size, 0), pltpu.roll(swapped, size, 0))
+            joined.append(jnp.where(lower, x, y) + moved)
+        arrays = joined
+    return arrays[0]
 
 
 def radiate(
@@ -334,7 +348,11 @@
             for b in range(2):
                 cols = columns(pair, b)
                 net[b, 0] = jnp.sum(top[...] * (1.0 - climbing[b]), axis=0)
-                total = jnp.sum(net[b], axis=1)
+                total = jnp.concatenate(
+                    [sublane_sums([net[b, 8 * k + i] for i in range(8)]) for k in range(LEV // 8)]
+                    + [jnp.sum(net[b, LEV], axis=0, keepdims=True)],
+                    axis=0,
+                )
                 heat = (total[:LEV] - total[1:]) * (72.0 * mu_ref[0:1, cols])
                 out_ref[:, cols] = jnp.where(lit_ref[0:1, cols] == 1, heat, 0.0)
 

time: 42.7 us -> 42.2 us (0.988)
  the two profiles are of different devices: /device:TPU:32 before, /device:TPU:0 now
where the time goes in v6:
time: 42.2 us; the launch traced here: 42 us
  Pallas kernels  41.4 us (98%)
  between operations  0.64 us (2%)
    pallas_call x1, Pallas kernels, shards(): pl.pallas_call(radiate, in_specs=[anywhere] + [vmem] * 6 + [anywhere], ou...  24.4 us
    pallas_call x1, Pallas kernels, shards(): pl.pallas_call(exchange, in_specs=[anywhere] * 3, out_specs=[anywhere, vm...  16.9 us

profile of v6, /device:TPU:0, one launch (start us, length us, event | category | flops | bytes accessed | tf_op | source)
XLA Modules:
  0.0 42.0 jit_solution(12065792640781011327)
XLA Ops:
  0.6 16.9 %exchange.1 = (f32[1152,1024]{1,0:T(8,128)}, f32[72,1024]{1,0:T(8,128)}) custom-call(f32[1152,1024]{1,0:T(8,128)} %bitcast.9, f32[1,1024]{1,0:T(1,128)} %bitcast.11, s32[2,1024]{1,0:T(2,128)} %partner_hbm.1), custom_call_target="tpu_custom_call" | custom-call | tf_op jit(solution)/shard_map/exchange/pallas_call | solution.py:400
  17.6 24.4 %radiate.1 = (f32[72,1024]{1,0:T(8,128)}, f32[1152,1024]{1,0:T(8,128)}) custom-call(f32[72,1024]{1,0:T(8,128)} %get-tuple-element.6.q_hbm, f32[1,1024]{1,0:T(1,128)} %bitcast.12, f32[1,1024]{1,0:T(1,128)} %bitcast.13, s32[1,1024]{1,0:T(1,128)} %bitcast.14, f32[72,112]{1,0:T(8,128)} %bitcast.10, f32[1,112]{1,0:T(1,128)} %bitcast.15, f32[1,112]{1,0:T(1,128)} %bitcast.16, ...), custom_call_target="tpu_custom_call" | custom-call | tf_op jit(solution)/shard_map/radiate/pallas_call | solution.py:424

commit v7 on v6

--- a/solution.py
+++ b/solution.py
@@ -81,10 +81,11 @@
     ]
     for copy in small:
         copy.start()
-    for group in range(AHEAD):
-        fetch(group).start()
+    fetch(0).start()
     for copy in small:
         copy.wait()
+    for group in range(1, AHEAD):
+        fetch(group).start()
     for block in range(blocks):
         cols = pl.ds(block * LANES, LANES)
         own = jnp.broadcast_to(j_ref[:, cols], (8, LANES))
@@ -131,8 +132,8 @@
     first_part(0)
     pl.semaphore_wait(barrier, 2)
     for way in range(2):
+        send(way, 0).start()
         send_jacobian(way).start()
-        send(way, 0).start()
     for group in range(AHEAD, AHEAD + 1):
         fetch(group).start()
 

time: 42.2 us -> 42.2 us (level)
  no operation moved by 1% of the time
where the time goes in v7:
time: 42.2 us; the launch traced here: 42 us
  Pallas kernels  41.4 us (98%)
  between operations  0.64 us (2%)
    pallas_call x1, Pallas kernels, shards(): pl.pallas_call(radiate, in_specs=[anywhere] + [vmem] * 6 + [anywhere], ou...  24.4 us
    pallas_call x1, Pallas kernels, shards(): pl.pallas_call(exchange, in_specs=[anywhere] * 3, out_specs=[anywhere, vm...  16.9 us

profile of v7, /device:TPU:0, one launch (start us, length us, event | category | flops | bytes accessed | tf_op | source)
XLA Modules:
  0.0 42.0 jit_solution(17068543474626636991)
XLA Ops:
  0.6 16.9 %exchange.1 = (f32[1152,1024]{1,0:T(8,128)}, f32[72,1024]{1,0:T(8,128)}) custom-call(f32[1152,1024]{1,0:T(8,128)} %bitcast.9, f32[1,1024]{1,0:T(1,128)} %bitcast.11, s32[2,1024]{1,0:T(2,128)} %partner_hbm.1), custom_call_target="tpu_custom_call" | custom-call | tf_op jit(solution)/shard_map/exchange/pallas_call | solution.py:401
  17.6 24.4 %radiate.1 = (f32[72,1024]{1,0:T(8,128)}, f32[1152,1024]{1,0:T(8,128)}) custom-call(f32[72,1024]{1,0:T(8,128)} %get-tuple-element.6.q_hbm, f32[1,1024]{1,0:T(1,128)} %bitcast.12, f32[1,1024]{1,0:T(1,128)} %bitcast.13, s32[1,1024]{1,0:T(1,128)} %bitcast.14, f32[72,112]{1,0:T(8,128)} %bitcast.10, f32[1,112]{1,0:T(1,128)} %bitcast.15, f32[1,112]{1,0:T(1,128)} %bitcast.16, ...), custom_call_target="tpu_custom_call" | custom-call | tf_op jit(solution)/shard_map/radiate/pallas_call | solution.py:425
